TPU v7x, 256 devices: a whole 4x4x8 slice. The times are simulated.
256 devices in a mesh: gx: 32 (over y, x, core), gy: 8 (over z).
Axes of the slice: x: 4, y: 4, z: 8, core: 2. Of those that a mesh axis runs over, the one named last changes fastest.
Arguments:
- initial_guess: float32 [16, 512, 16384], P(None, 'gx', 'gy')
- conductivity: float32 [512, 16384], P('gx', 'gy'), may hold values from 0.05 to 0.5
- electrodes: int32 [16], replicated, may hold values from 0 to 8388607
Outputs:
- basis: float32 [48, 512, 16384], P(None, 'gx', 'gy')
- triangle: float32 [48, 48], replicated
Inputs may be any that keep to these rules, and one draw needn't show every extreme that they name: `electrodes`: each entry is a flattened cell index (x * 256 + y) * 64 + z.
All inputs are finite; a program needn't handle non-finite values.
Results may differ from a plain program's by a relative error of at most 0.0003.
Values sent between devices are 32-bit elements; how exact they have to be, the bound alone decides.
A program may use at most 128 MiB of HBM per device.

v0:
```python
import math

import jax
import jax.numpy as jnp
from jax import lax
from jax.sharding import PartitionSpec as P

NZ = 64


NEIGHBOURS = ((2, 1, 1), (0, 1, 1), (1, 2, 1), (1, 0, 1), (1, 1, 2), (1, 1, 0))


def with_halo(cells, sides, width):
    for axis, dim in sides:
        count = lax.axis_size(axis)
        ends = count - 1
        head = lax.slice_in_dim(cells, 0, width, axis=dim)
        tail = lax.slice_in_dim(cells, cells.shape[dim] - width, cells.shape[dim], axis=dim)
        cells = jnp.concatenate(
            [
                lax.ppermute(tail, axis, [(i, (i + 1) % count) for i in range(ends)]),
                cells,
                lax.ppermute(head, axis, [((i + 1) % count, i) for i in range(ends)]),
            ],
            axis=dim,
        )
    return cells


def window(values, starts):
    base = values.ndim - 3
    result = values
    for offset, anchor in enumerate(starts):
        axis_number = base + offset
        extent = values.shape[axis_number]
        result = lax.slice_in_dim(result, anchor, anchor + extent - 2, axis=axis_number)
    return result


def stencil(padded_field, padded_cond):
    centre = padded_field[:, 1:-1, 1:-1, 1:-1]
    cond_centre = padded_cond[1:-1, 1:-1, 1:-1]
    total = jnp.zeros_like(centre)
    for starts in NEIGHBOURS:
        coupling = 0.5 * (cond_centre + window(padded_cond, starts))
        total = total + coupling * (centre - window(padded_field, starts))
    return total


def apply_rimmed(field, cond):
    padded_field = jnp.pad(field, ((0, 0), (0, 0), (0, 0), (1, 1)))
    padded_cond = jnp.pad(cond, ((0, 0), (0, 0), (1, 1)))
    return stencil(padded_field, padded_cond)


def point_sources(electrodes, cells_x, cells_y, depth, width):
    total_y = cells_y * lax.axis_size("gy")
    coord_x = (
        lax.axis_index("gx") * cells_x - width + jnp.arange(cells_x + 2 * width, dtype=jnp.int32)
    )
    coord_y = (
        lax.axis_index("gy") * cells_y - width + jnp.arange(cells_y + 2 * width, dtype=jnp.int32)
    )
    coord_z = jnp.arange(depth, dtype=jnp.int32)
    flat_index = (coord_x[:, None, None] * total_y + coord_y[None, :, None]) * depth + coord_z[
        None, None, :
    ]
    hits = flat_index[None] == electrodes[:, None, None, None]
    return 20.0 * hits.astype(jnp.float32)


def field_power(field, cond_rim):
    rimmed = with_halo(field, (("gx", 1), ("gy", 2)), 1)
    return apply_rimmed(rimmed, cond_rim)


def per_device(initial_guess, conductivity, electrodes):
    sources, cells_x, merged = initial_guess.shape
    depth = NZ
    cells_y = merged // depth
    guess_grid = initial_guess.reshape(sources, cells_x, cells_y, depth)
    cond_grid = conductivity.reshape(cells_x, cells_y, depth)
    stacked = jnp.concatenate([guess_grid, cond_grid[None]], 0)
    extended = with_halo(stacked, (("gx", 1), ("gy", 2)), 1)
    field_one = extended[:sources]
    cond_one = extended[sources]
    source_field = point_sources(electrodes, cells_x, cells_y, depth, 0)
    first = source_field - apply_rimmed(field_one, cond_one)
    second = field_power(first, cond_one) - 0.8 * first
    third = field_power(second, cond_one) - 1.6 * second
    count = 3 * sources
    columns = jnp.concatenate([first, second, third], 0).reshape(count, cells_x * cells_y * depth)
    local_gram = jnp.dot(columns, columns.T, precision=lax.Precision.HIGHEST)
    gram = lax.psum(local_gram, ("gx", "gy"))
    lower = jnp.linalg.cholesky(gram)
    cells = cells_x * lax.axis_size("gx") * cells_y * lax.axis_size("gy") * depth
    scale = math.sqrt(cells)
    solved = jax.scipy.linalg.solve_triangular(lower, columns, lower=True)
    basis = (solved * scale).reshape(count, cells_x, cells_y * depth)
    triangle = lower.T / scale
    return (basis, triangle)


def solution(mesh):
    return jax.shard_map(
        per_device,
        mesh=mesh,
        in_specs=(P(None, "gx", "gy"), P("gx", "gy"), P()),
        out_specs=(P(None, "gx", "gy"), P()),
        check_vma=False,
    )
```

profile of v0, /device:TPU:1, one launch (start us, length us, event | category | flops | bytes accessed | tf_op | source)
XLA Modules:
  0.0 279.2 jit_solution(10238517785658662273)
XLA Ops:
  0.6 1.2 broadcast_in_dim_reshape.3
  1.9 4.9 %reshape.77 = f32[16,16,32,64]{3,2,1,0:T(8,128)} reshape(f32[16,16,2048]{2,1,0:T(8,128)} %param.3) | data formatting | bytes 4194304 | tf_op jit(solution)/shard_map/reshape | solution.py:82
  6.8 7.5 %copy_dynamic-update-slice_fusion = f32[17,16,32,64]{3,0,2,1:T(8,128)} fusion(f32[16,16,32,64]{3,2,1,0:T(8,128)} %reshape.77), kind=kLoop, calls=%fused_computation.95 | loop fusion | bytes 6291456
  14.2 7.9 %dynamic-update-slice.4 = f32[17,16,32,64]{3,0,2,1:T(8,128)} dynamic-update-slice(f32[17,16,32,64]{3,0,2,1:T(8,128)} %copy_dynamic-update-slice_fusion, f32[1,16,32,64]{3,0,2,1:T(1,128)S(1)} %broadcast_in_dim_reshape.3, s32[]{} %constant.105, s32[]{} %constant.104, s32[]{} %constant.104, s32[]{} %constant.104) | dynamic-update-slice | bytes 262148 | tf_op jit(solution)/shard_map/concatenate | solution.py:84
  22.1 1.2 fusion.59
  23.3 4.5 %collective-permute-start = (f32[17,1,32,64]{3,0,2,1:T(8,128)S(1)}, f32[17,1,32,64]{3,0,2,1:T(8,128)S(1)}, u32[]{:S(2)}, u32[]{:S(2)}) collective-permute-start(f32[17,1,32,64]{3,0,2,1:T(8,128)S(1)} %get-tuple-element.8), channel_id=1, source_target_pairs={{0,8},{8,16},{16,24},{24,32},{32,40},{40,48},{48,56},{56,64},{64,7... | collective-permute-start | bytes 417800 | tf_op jit(solution)/shard_map/ppermute | solution.py:22
  27.8 2.0 collective-permute-start.1
  29.9 2.6 collective-permute-done
  32.5 4.4 %collective-permute-done.1 = f32[17,1,32,64]{3,0,2,1:T(8,128)S(1)} collective-permute-done((f32[17,1,32,64]{3,0,2,1:T(8,128)S(1)}, f32[17,1,32,64]{3,0,2,1:T(8,128)S(1)}, u32[]{:S(2)}, u32[]{:S(2)}) %collective-permute-start.1) | collective-permute-done | bytes 139296 | tf_op jit(solution)/shard_map/ppermute | solution.py:24
  36.9 1.1 pad_maximum_fusion.28
  37.9 3.6 %collective-permute-start.2 = (f32[17,18,1,64]{3,0,2,1:T(8,128)S(1)}, f32[17,18,1,64]{3,0,2,1:T(8,128)S(1)}, u32[]{:S(2)}, u32[]{:S(2)}) collective-permute-start(f32[17,18,1,64]{3,0,2,1:T(8,128)S(1)} %get-tuple-element.6), channel_id=1, source_target_pairs={{0,1},{1,2},{2,3},{3,4},{4,5},{5,6},{6,7},{8,9},{9,10},{10,11},{11... | collective-permute-start | bytes 235016 | tf_op jit(solution)/shard_map/ppermute | solution.py:22
  41.5 1.3 collective-permute-start.3
  42.9 1.4 collective-permute-done.2
  44.3 4.0 %collective-permute-done.3 = f32[17,18,1,64]{3,0,2,1:T(8,128)S(1)} collective-permute-done((f32[17,18,1,64]{3,0,2,1:T(8,128)S(1)}, f32[17,18,1,64]{3,0,2,1:T(8,128)S(1)}, u32[]{:S(2)}, u32[]{:S(2)}) %collective-permute-start.3) | collective-permute-done | bytes 78368 | tf_op jit(solution)/shard_map/ppermute | solution.py:24
  48.9 2.7 select_maximum_fusion.8
  51.7 9.4 %fusion.35 = f32[16,16,32,64]{3,0,2,1:T(8,128)S(1)} fusion(f32[16,18,34,66]{3,0,2,1:T(8,128)S(1)} %select_maximum_fusion.8, f32[17,18,1,64]{3,0,2,1:T(8,128)S(1)} %collective-permute-done.2, f32[17,1,32,64]{3,0,2,1:T(8,128)S(1)} %collective-permute-done.1, f32[17,16,32,64]{3,0,2,1:T(8,128)S(1)} %copy-done, f32[17,1,32,64]{3,0,2,1:T(8,128)S(1)} %collective-permute-done, ...), kind=kLoop, calls=%fused_computation.72 | loop fusion | flops 14680064 | bytes 11969600 | tf_op jit(solution)/shard_map/sub | solution.py:89
  61.1 4.7 %collective-permute-start.5 = (f32[16,1,32,64]{3,0,2,1:T(8,128)S(1)}, f32[16,1,32,64]{3,0,2,1:T(8,128)S(1)}, u32[]{:S(2)}, u32[]{:S(2)}) collective-permute-start(f32[16,1,32,64]{3,0,2,1:T(8,128)S(1)} %get-tuple-element.16), channel_id=1, source_target_pairs={{0,8},{8,16},{16,24},{24,32},{32,40},{40,48},{48,56},{56,64},{64,7... | collective-permute-start | bytes 393224 | tf_op jit(solution)/shard_map/ppermute | solution.py:22
  65.9 1.9 collective-permute-start.4
  67.8 1.4 collective-permute-done.5
  69.2 4.4 %collective-permute-done.4 = f32[16,1,32,64]{3,0,2,1:T(8,128)S(1)} collective-permute-done((f32[16,1,32,64]{3,0,2,1:T(8,128)S(1)}, f32[16,1,32,64]{3,0,2,1:T(8,128)S(1)}, u32[]{:S(2)}, u32[]{:S(2)}) %collective-permute-start.4) | collective-permute-done | bytes 131104 | tf_op jit(solution)/shard_map/ppermute | solution.py:24
  73.6 3.5 %collective-permute-start.7 = (f32[16,18,1,64]{3,0,2,1:T(8,128)S(1)}, f32[16,18,1,64]{3,0,2,1:T(8,128)S(1)}, u32[]{:S(2)}, u32[]{:S(2)}) collective-permute-start(f32[16,18,1,64]{3,0,2,1:T(8,128)S(1)} %get-tuple-element.12), channel_id=1, source_target_pairs={{0,1},{1,2},{2,3},{3,4},{4,5},{5,6},{6,7},{8,9},{9,10},{10,11},{11... | collective-permute-start | bytes 221192 | tf_op jit(solution)/shard_map/ppermute | solution.py:22
  77.1 1.5 collective-permute-start.6
  78.6 0.6 collective-permute-done.7
  79.2 5.0 %collective-permute-done.6 = f32[16,18,1,64]{3,0,2,1:T(8,128)S(1)} collective-permute-done((f32[16,18,1,64]{3,0,2,1:T(8,128)S(1)}, f32[16,18,1,64]{3,0,2,1:T(8,128)S(1)}, u32[]{:S(2)}, u32[]{:S(2)}) %collective-permute-start.6) | collective-permute-done | bytes 73760 | tf_op jit(solution)/shard_map/ppermute | solution.py:24
  84.2 2.7 select_maximum_fusion.4
  86.9 5.6 %fusion.19 = f32[16,16,32,64]{3,0,2,1:T(8,128)S(1)} fusion(f32[16,16,32,64]{3,0,2,1:T(8,128)S(1)} %fusion.35, f32[16,18,34,66]{3,0,2,1:T(8,128)S(1)} %select_maximum_fusion.4, f32[16,18,1,64]{3,0,2,1:T(8,128)S(1)} %collective-permute-done.7, f32[16,1,32,64]{3,0,2,1:T(8,128)S(1)} %collective-permute-done.4, f32[16,1,32,64]{3,0,2,1:T(8,128)S(1)} %collective-permute-done.5, ...), kind=kLoop, calls=%fused_computation.46 | loop fusion | flops 14155776 | bytes 9584640 | tf_op jit(solution)/shard_map/sub | solution.py:90
  92.6 3.3 %collective-permute-start.9 = (f32[16,1,32,64]{3,0,2,1:T(8,128)S(1)}, f32[16,1,32,64]{3,0,2,1:T(8,128)S(1)}, u32[]{:S(2)}, u32[]{:S(2)}) collective-permute-start(f32[16,1,32,64]{3,0,2,1:T(8,128)S(1)} %get-tuple-element.14), channel_id=1, source_target_pairs={{0,8},{8,16},{16,24},{24,32},{32,40},{40,48},{48,56},{56,64},{64,7... | collective-permute-start | bytes 393224 | tf_op jit(solution)/shard_map/ppermute | solution.py:22
  95.9 1.9 collective-permute-start.8
  97.8 1.4 collective-permute-done.9
  99.2 4.4 %collective-permute-done.8 = f32[16,1,32,64]{3,0,2,1:T(8,128)S(1)} collective-permute-done((f32[16,1,32,64]{3,0,2,1:T(8,128)S(1)}, f32[16,1,32,64]{3,0,2,1:T(8,128)S(1)}, u32[]{:S(2)}, u32[]{:S(2)}) %collective-permute-start.8) | collective-permute-done | bytes 131104 | tf_op jit(solution)/shard_map/ppermute | solution.py:24
  103.6 5.3 %collective-permute-start.11 = (f32[16,18,1,64]{3,0,2,1:T(8,128)S(1)}, f32[16,18,1,64]{3,0,2,1:T(8,128)S(1)}, u32[]{:S(2)}, u32[]{:S(2)}) collective-permute-start(f32[16,18,1,64]{3,0,2,1:T(8,128)S(1)} %get-tuple-element.10), channel_id=1, source_target_pairs={{0,1},{1,2},{2,3},{3,4},{4,5},{5,6},{6,7},{8,9},{9,10},{10,11},{11... | collective-permute-start | bytes 221192 | tf_op jit(solution)/shard_map/ppermute | solution.py:22
  108.9 1.3 collective-permute-start.10
  110.2 0.8 collective-permute-done.11
  111.0 4.4 %collective-permute-done.10 = f32[16,18,1,64]{3,0,2,1:T(8,128)S(1)} collective-permute-done((f32[16,18,1,64]{3,0,2,1:T(8,128)S(1)}, f32[16,18,1,64]{3,0,2,1:T(8,128)S(1)}, u32[]{:S(2)}, u32[]{:S(2)}) %collective-permute-start.10) | collective-permute-done | bytes 73760 | tf_op jit(solution)/shard_map/ppermute | solution.py:24
  115.4 2.7 select_maximum_fusion
  118.1 6.7 %fusion.3 = f32[16,16,32,64]{3,0,2,1:T(8,128)} fusion(f32[16,16,32,64]{3,0,2,1:T(8,128)S(1)} %fusion.19, f32[16,18,34,66]{3,0,2,1:T(8,128)S(1)} %select_maximum_fusion, f32[16,18,1,64]{3,0,2,1:T(8,128)S(1)} %collective-permute-done.11, f32[16,1,32,64]{3,0,2,1:T(8,128)S(1)} %collective-permute-done.8, f32[16,1,32,64]{3,0,2,1:T(8,128)S(1)} %collective-permute-done.9, ...), kind=kLoop, calls=%fused_computation.20 | loop fusion | flops 14155776 | bytes 9584640 | tf_op jit(solution)/shard_map/sub | solution.py:91
  124.8 16.2 %convolution_bitcast_fusion = f32[48,48]{0,1:T(8,128)S(1)} fusion(f32[16,16,32,64]{3,0,2,1:T(8,128)} %fusion.3, f32[16,16,32,64]{3,0,2,1:T(8,128)} %copy-done.2, f32[16,16,32,64]{3,0,2,1:T(8,128)} %copy-done.1), kind=kOutput, calls=%fused_computation.96 | convolution fusion | flops 909115392 | bytes 6300672 | tf_op jit(solution)/shard_map/dot_general | solution.py:94
  141.0 10.2 %pad_maximum_fusion = f32[48,16,32,64]{3,0,2,1:T(8,128)} fusion(f32[16,16,32,64]{3,0,2,1:T(8,128)} %fusion.3, f32[16,16,32,64]{3,0,2,1:T(8,128)} %copy-done.2, f32[16,16,32,64]{3,0,2,1:T(8,128)} %copy-done.1), kind=kLoop, calls=%fused_computation.1 | loop fusion | flops 3145728 | bytes 12582912 | tf_op jit(solution)/shard_map/concatenate | solution.py:93
  151.2 80.4 %psum.7 = f32[48,48]{0,1:T(8,128)S(1)} all-reduce(f32[48,48]{0,1:T(8,128)S(1)} %convolution_bitcast_fusion), channel_id=1, replica_groups=mesh['gx'=32,'gy'=8] {'gx','gy'}, use_global_device_ids=true, to_apply=%region_0.1 | all-reduce | flops 2304 | bytes 18432 | tf_op jit(solution)/shard_map/psum | solution.py:95
  231.6 13.1 %copy.17 = f32[48,16,32,64]{3,2,1,0:T(8,128)} copy(f32[48,16,32,64]{3,0,2,1:T(8,128)} %pad_maximum_fusion) | data formatting | bytes 12582912 | tf_op jit(solution)/shard_map/concatenate | solution.py:93
  244.7 9.9 %reshape.78 = f32[48,32768]{1,0:T(8,128)} reshape(f32[48,16,32,64]{3,2,1,0:T(8,128)} %copy.17) | data formatting | bytes 12582912 | tf_op jit(solution)/shard_map/reshape | solution.py:93
  254.7 4.4 %cholesky.16 = f32[48,48]{1,0:T(8,128)S(1)} custom-call(f32[48,48]{1,0:T(8,128)S(1)} %fusion.58), custom_call_target="Cholesky" | custom-call | tf_op jit(solution)/shard_map/jit(cholesky)/cholesky | solution.py:96
  259.1 0.6 compare_reduce_fusion
  259.8 0.7 multiply_bitcast_fusion
  260.4 0.7 copy.18
  261.1 3.7 %custom-call.7 = f32[1,48,48]{1,2,0:T(8,128)S(1)} custom-call(f32[1,48,48]{2,1,0:T(8,128)S(1)} %get-tuple-element.25), custom_call_target="InvertDiagBlocksLowerTriangular" | custom-call | tf_op jit(solution)/shard_map/jit(_solve_triangular)/triangular_solve | solution.py:99
  264.8 8.2 %convolution_multiply_fusion = f32[48,32768]{1,0:T(8,128)S(1)} fusion(f32[48,32768]{1,0:T(8,128)} %reshape.78, f32[1,48,48]{1,2,0:T(8,128)S(1)} %custom-call.7), kind=kOutput, calls=%fused_computation | convolution fusion | flops 907542528 | bytes 12592128 | tf_op jit(solution)/shard_map/jit(_solve_triangular)/triangular_solve | solution.py:99
  273.0 6.3 %copy.22 = f32[6,8,16,2048]{3,2,1,0:T(8,128)} copy(f32[6,8,16,2048]{3,1,2,0:T(8,128)S(1)} %bitcast.21) | data formatting | bytes 12582912
  (24 shorter events, 1.0 us)
Async XLA Ops:
  23.3 9.2 %collective-permute-start = (f32[17,1,32,64]{3,0,2,1:T(8,128)S(1)}, f32[17,1,32,64]{3,0,2,1:T(8,128)S(1)}, u32[]{:S(2)}, u32[]{:S(2)}) collective-permute-start(f32[17,1,32,64]{3,0,2,1:T(8,128)S(1)} %get-tuple-element.8), channel_id=1, source_target_pairs={{0,8},{8,16},{16,24},{24,32},{32,40},{40,48},{48,56},{56,64},{64,7... | collective-permute-start | bytes 417800 | tf_op jit(solution)/shard_map/ppermute | solution.py:22
  27.8 9.1 %collective-permute-start.1 = (f32[17,1,32,64]{3,0,2,1:T(8,128)S(1)}, f32[17,1,32,64]{3,0,2,1:T(8,128)S(1)}, u32[]{:S(2)}, u32[]{:S(2)}) collective-permute-start(f32[17,1,32,64]{3,0,2,1:T(8,128)S(1)} %get-tuple-element.9), channel_id=1, source_target_pairs={{8,0},{16,8},{24,16},{32,24},{40,32},{48,40},{56,48},{64,56},{72,6... | collective-permute-start | bytes 417800 | tf_op jit(solution)/shard_map/ppermute | solution.py:24
  29.8 18.6 %copy-start = (f32[17,16,32,64]{3,0,2,1:T(8,128)S(1)}, f32[17,16,32,64]{3,0,2,1:T(8,128)}, u32[]{:S(2)}) copy-start(f32[17,16,32,64]{3,0,2,1:T(8,128)} %dynamic-update-slice.4) | copy-start | bytes 6684676
  37.9 6.4 %collective-permute-start.2 = (f32[17,18,1,64]{3,0,2,1:T(8,128)S(1)}, f32[17,18,1,64]{3,0,2,1:T(8,128)S(1)}, u32[]{:S(2)}, u32[]{:S(2)}) collective-permute-start(f32[17,18,1,64]{3,0,2,1:T(8,128)S(1)} %get-tuple-element.6), channel_id=1, source_target_pairs={{0,1},{1,2},{2,3},{3,4},{4,5},{5,6},{6,7},{8,9},{9,10},{10,11},{11... | collective-permute-start | bytes 235016 | tf_op jit(solution)/shard_map/ppermute | solution.py:22
  41.5 6.9 %collective-permute-start.3 = (f32[17,18,1,64]{3,0,2,1:T(8,128)S(1)}, f32[17,18,1,64]{3,0,2,1:T(8,128)S(1)}, u32[]{:S(2)}, u32[]{:S(2)}) collective-permute-start(f32[17,18,1,64]{3,0,2,1:T(8,128)S(1)} %get-tuple-element.7), channel_id=1, source_target_pairs={{1,0},{2,1},{3,2},{4,3},{5,4},{6,5},{7,6},{9,8},{10,9},{11,10},{12... | collective-permute-start | bytes 235016 | tf_op jit(solution)/shard_map/ppermute | solution.py:24
  48.9 2.8 copy-start.3
  48.9 2.8 copy-start.4
  61.1 25.8 %copy-start.1 = (f32[16,16,32,64]{3,0,2,1:T(8,128)}, f32[16,16,32,64]{3,0,2,1:T(8,128)S(1)}, u32[]{:S(2)}) copy-start(f32[16,16,32,64]{3,0,2,1:T(8,128)S(1)} %fusion.35) | copy-start | bytes 6291460
  61.1 8.0 %collective-permute-start.5 = (f32[16,1,32,64]{3,0,2,1:T(8,128)S(1)}, f32[16,1,32,64]{3,0,2,1:T(8,128)S(1)}, u32[]{:S(2)}, u32[]{:S(2)}) collective-permute-start(f32[16,1,32,64]{3,0,2,1:T(8,128)S(1)} %get-tuple-element.16), channel_id=1, source_target_pairs={{0,8},{8,16},{16,24},{24,32},{32,40},{40,48},{48,56},{56,64},{64,7... | collective-permute-start | bytes 393224 | tf_op jit(solution)/shard_map/ppermute | solution.py:22
  65.9 7.7 %collective-permute-start.4 = (f32[16,1,32,64]{3,0,2,1:T(8,128)S(1)}, f32[16,1,32,64]{3,0,2,1:T(8,128)S(1)}, u32[]{:S(2)}, u32[]{:S(2)}) collective-permute-start(f32[16,1,32,64]{3,0,2,1:T(8,128)S(1)} %get-tuple-element.17), channel_id=1, source_target_pairs={{8,0},{16,8},{24,16},{32,24},{40,32},{48,40},{56,48},{64,56},{72,6... | collective-permute-start | bytes 393224 | tf_op jit(solution)/shard_map/ppermute | solution.py:24
  73.6 5.6 %collective-permute-start.7 = (f32[16,18,1,64]{3,0,2,1:T(8,128)S(1)}, f32[16,18,1,64]{3,0,2,1:T(8,128)S(1)}, u32[]{:S(2)}, u32[]{:S(2)}) collective-permute-start(f32[16,18,1,64]{3,0,2,1:T(8,128)S(1)} %get-tuple-element.12), channel_id=1, source_target_pairs={{0,1},{1,2},{2,3},{3,4},{4,5},{5,6},{6,7},{8,9},{9,10},{10,11},{11... | collective-permute-start | bytes 221192 | tf_op jit(solution)/shard_map/ppermute | solution.py:22
  77.1 7.1 %collective-permute-start.6 = (f32[16,18,1,64]{3,0,2,1:T(8,128)S(1)}, f32[16,18,1,64]{3,0,2,1:T(8,128)S(1)}, u32[]{:S(2)}, u32[]{:S(2)}) collective-permute-start(f32[16,18,1,64]{3,0,2,1:T(8,128)S(1)} %get-tuple-element.13), channel_id=1, source_target_pairs={{1,0},{2,1},{3,2},{4,3},{5,4},{6,5},{7,6},{9,8},{10,9},{11,10},{12... | collective-permute-start | bytes 221192 | tf_op jit(solution)/shard_map/ppermute | solution.py:24
  92.5 25.6 %copy-start.2 = (f32[16,16,32,64]{3,0,2,1:T(8,128)}, f32[16,16,32,64]{3,0,2,1:T(8,128)S(1)}, u32[]{:S(2)}) copy-start(f32[16,16,32,64]{3,0,2,1:T(8,128)S(1)} %fusion.19) | copy-start | bytes 6291460
  92.6 6.6 %collective-permute-start.9 = (f32[16,1,32,64]{3,0,2,1:T(8,128)S(1)}, f32[16,1,32,64]{3,0,2,1:T(8,128)S(1)}, u32[]{:S(2)}, u32[]{:S(2)}) collective-permute-start(f32[16,1,32,64]{3,0,2,1:T(8,128)S(1)} %get-tuple-element.14), channel_id=1, source_target_pairs={{0,8},{8,16},{16,24},{24,32},{32,40},{40,48},{48,56},{56,64},{64,7... | collective-permute-start | bytes 393224 | tf_op jit(solution)/shard_map/ppermute | solution.py:22
  95.9 7.7 %collective-permute-start.8 = (f32[16,1,32,64]{3,0,2,1:T(8,128)S(1)}, f32[16,1,32,64]{3,0,2,1:T(8,128)S(1)}, u32[]{:S(2)}, u32[]{:S(2)}) collective-permute-start(f32[16,1,32,64]{3,0,2,1:T(8,128)S(1)} %get-tuple-element.15), channel_id=1, source_target_pairs={{8,0},{16,8},{24,16},{32,24},{40,32},{48,40},{56,48},{64,56},{72,6... | collective-permute-start | bytes 393224 | tf_op jit(solution)/shard_map/ppermute | solution.py:24
  103.6 7.4 %collective-permute-start.11 = (f32[16,18,1,64]{3,0,2,1:T(8,128)S(1)}, f32[16,18,1,64]{3,0,2,1:T(8,128)S(1)}, u32[]{:S(2)}, u32[]{:S(2)}) collective-permute-start(f32[16,18,1,64]{3,0,2,1:T(8,128)S(1)} %get-tuple-element.10), channel_id=1, source_target_pairs={{0,1},{1,2},{2,3},{3,4},{4,5},{5,6},{6,7},{8,9},{9,10},{10,11},{11... | collective-permute-start | bytes 221192 | tf_op jit(solution)/shard_map/ppermute | solution.py:22
  108.9 6.5 %collective-permute-start.10 = (f32[16,18,1,64]{3,0,2,1:T(8,128)S(1)}, f32[16,18,1,64]{3,0,2,1:T(8,128)S(1)}, u32[]{:S(2)}, u32[]{:S(2)}) collective-permute-start(f32[16,18,1,64]{3,0,2,1:T(8,128)S(1)} %get-tuple-element.11), channel_id=1, source_target_pairs={{1,0},{2,1},{3,2},{4,3},{5,4},{6,5},{7,6},{9,8},{10,9},{11,10},{12... | collective-permute-start | bytes 221192 | tf_op jit(solution)/shard_map/ppermute | solution.py:24
where the time goes:
time: 280 us; the launch traced here: 279 us
  blocking collectives  80.4 us (29%)
  local copies, waits for them, and re-layouts  52.7 us (19%)
  other arithmetic  51.2 us (18%)
  starting transfers between devices  34.8 us (12%)
  waiting for transfers between devices  34.7 us (12%)
  matrix products  24.4 us (9%)
    psum x1, blocking collectives, per_device(): gram = lax.psum(local_gram, ('gx', 'gy'))  80.4 us
    ppermute x6, waiting for transfers between devices, with_halo(): lax.ppermute(head, axis, [((i + 1) % count, i) for i in range(ends)])  26.6 us
    ppermute x6, starting transfers between devices, with_halo(): lax.ppermute(tail, axis, [(i, (i + 1) % count) for i in range(ends)])  24.9 us
    dot_general x1, matrix products, per_device(): local_gram = jnp.dot(columns, columns.T, precision=lax.Precision.HIGHEST)  16.2 us
    unnamed x14, local copies, waits for them, and re-layouts  14.5 us
    concatenate x1, local copies, waits for them, and re-layouts, per_device(): jnp.concatenate([first, second, third], 0)  13.1 us
    concatenate x1, other arithmetic, per_device(): jnp.concatenate([first, second, third], 0)  10.2 us
    reshape x1, local copies, waits for them, and re-layouts, per_device(): jnp.concatenate([first, second, third], 0)  9.86 us
  transfers between devices with their start and end apart: 12, of which 12 were waited for; matrix products, arithmetic and copies ran while one was open for 0% of the time, Pallas kernels for 0%

commit v1 on v0

v1 whole, which is shorter than its diff:
```python
import functools
import math

import jax
import jax.numpy as jnp
from jax import lax
from jax.experimental import pallas as pl
from jax.experimental.pallas import tpu as pltpu
from jax.sharding import PartitionSpec as P

MESH = pl.DeviceIdType.MESH
NZ = 64
LANES = 128
HALF = 64
SRC = 16
COLS = 48
CX = 16
TILES = 16
REACH = 3
EXT_X = CX + 2 * REACH
EXT_T = TILES + 2
EXT = EXT_T * LANES
MERGED = TILES * LANES
GX, GY = 32, 8
MOVES = ((1, 0), (-1, 0), (0, 1), (0, -1), (1, 1), (1, -1), (-1, 1), (-1, -1))


def tile(t):
    if isinstance(t, int):
        return pl.ds(t * LANES, LANES)
    return pl.ds(pl.multiple_of(t * LANES, LANES), LANES)


def swap_halves(v):
    return pltpu.roll(v, HALF, 1)


def partner(kind, gx, gy, step):
    if kind == 0:
        base = (gx // 8) * 8
        return (base + lax.rem(gx - base + step, 8), gy)
    if kind == 1:
        return (lax.rem(gx + 8 * step, GX), gy)
    return (gx, lax.rem(gy + step, GY))


def place(kind, gx, gy):
    return (lax.rem(gx, 8), gx // 8, gy)[kind]


GROUPS = (8, 4, 8)


def krylov_kernel(
    guess,
    cond,
    electrodes,
    cols,
    gram,
    natural,
    start,
    field,
    cond_ext,
    coef,
    third_out,
    third_in,
    split,
    part0,
    part1,
    part2,
    guess_sem,
    local_sem,
    cond_send,
    cond_recv,
    send,
    recv,
    third_send_sem,
    third_recv_sem,
    sum_send,
    sum_recv,
):
    gx, gy = lax.axis_index("gx"), lax.axis_index("gy")
    f32 = jnp.float32

    def beside(move):
        dx, dy = move
        return (lax.rem(gx + dx + GX, GX), lax.rem(gy + dy + GY, GY))

    loads = [
        pltpu.make_async_copy(guess.at[:, tile(t)], natural.at[t], guess_sem.at[t])
        for t in range(TILES)
    ]
    for load in loads:
        load.start()
    load_cond = pltpu.make_async_copy(
        cond, cond_ext.at[pl.ds(8, CX), pl.ds(2 * LANES, MERGED)], local_sem.at[1]
    )
    load_cond.start()

    barrier = pltpu.get_barrier_semaphore()
    for move in MOVES:
        pl.semaphore_signal(barrier, inc=1, device_id=beside(move), device_id_type=MESH)
    for kind, size in enumerate(GROUPS):
        for step in range(1, size):
            pl.semaphore_signal(
                barrier, inc=1, device_id=partner(kind, gx, gy, step), device_id_type=MESH
            )

    for x in (0, EXT_X - 1):
        for t in (0, EXT_T - 1):
            start[x, :, tile(t)] = jnp.zeros((SRC, LANES), f32)
    for x in (0, 8 + CX):
        for t in (0, EXT_T + 1):
            cond_ext[pl.ds(x, 8), tile(t)] = jnp.zeros((8, LANES), f32)

    for load in loads:
        load.wait()

    def lay_out(x, carry):
        for t in range(TILES):
            start[x + REACH, :, tile(t + 1)] = natural[t, pl.ds(x, SRC, stride=CX), :]
        return carry

    lax.fori_loop(0, CX, lay_out, 0)

    lane = lax.broadcasted_iota(jnp.int32, (SRC, LANES), 1)
    low = lane < HALF

    def pack_third(x, carry):
        near, far = REACH + x, REACH + CX // 2 + x
        third_out[0, x] = jnp.where(
            low, swap_halves(start[near, :, tile(TILES - 1)]), start[far, :, tile(TILES - 1)]
        )
        third_out[1, x] = jnp.where(
            low, start[far, :, tile(2)], swap_halves(start[near, :, tile(2)])
        )
        return carry

    lax.fori_loop(0, CX // 2, pack_third, 0)

    pl.semaphore_wait(barrier, len(MOVES) + sum(GROUPS) - len(GROUPS))

    cond_copies = []
    for i, (dx, dy) in enumerate(MOVES):
        if dx == 0:
            rows_from, rows_to, rows = pl.ds(0, CX), pl.ds(8, CX), CX
        elif dx > 0:
            rows_from, rows_to = pl.ds(CX - 8, 8), pl.ds(0, 8)
        else:
            rows_from, rows_to = pl.ds(0, 8), pl.ds(8 + CX, 8)
        if dy == 0:
            lanes_from, lanes_to = pl.ds(0, MERGED), pl.ds(2 * LANES, MERGED)
        elif dx == 0:
            lanes_from = pl.ds(MERGED - 2 * LANES if dy > 0 else 0, 2 * LANES)
            lanes_to = pl.ds(0 if dy > 0 else (TILES + 2) * LANES, 2 * LANES)
        else:
            lanes_from = tile(TILES - 1 if dy > 0 else 0)
            lanes_to = tile(1 if dy > 0 else TILES + 2)
        cond_copies.append(
            pltpu.make_async_remote_copy(
                src_ref=cond.at[rows_from, lanes_from],
                dst_ref=cond_ext.at[rows_to, lanes_to],
                send_sem=cond_send.at[i],
                recv_sem=cond_recv.at[i],
                device_id=beside((dx, dy)),
                device_id_type=MESH,
            )
        )
    copies = []
    for i, (dx, dy) in enumerate(MOVES):
        depth = REACH if dy == 0 else 2
        if dx == 0:
            x_from, x_to = pl.ds(REACH, CX), pl.ds(REACH, CX)
        elif dx > 0:
            x_from, x_to = pl.ds(REACH + CX - depth, depth), pl.ds(REACH - depth, depth)
        else:
            x_from, x_to = pl.ds(REACH, depth), pl.ds(REACH + CX, depth)
        if dy == 0:
            lanes_from = lanes_to = pl.ds(LANES, MERGED)
        else:
            lanes_from = tile(TILES if dy > 0 else 1)
            lanes_to = tile(0 if dy > 0 else TILES + 1)
        copies.append(
            pltpu.make_async_remote_copy(
                src_ref=start.at[x_from, :, lanes_from],
                dst_ref=start.at[x_to, :, lanes_to],
                send_sem=send.at[i],
                recv_sem=recv.at[i],
                device_id=beside((dx, dy)),
                device_id_type=MESH,
            )
        )
    thirds = [
        pltpu.make_async_remote_copy(
            src_ref=third_out.at[i],
            dst_ref=third_in.at[i],
            send_sem=third_send_sem.at[i],
            recv_sem=third_recv_sem.at[i],
            device_id=beside(move),
            device_id_type=MESH,
        )
        for i, move in enumerate(((0, 1), (0, -1)))
    ]
    for copy in cond_copies + copies + thirds:
        copy.start()

    load_cond.wait()
    for copy in cond_copies:
        copy.wait_recv()
    row = lax.broadcasted_iota(jnp.int32, (CX + 16, LANES), 0)
    lane_c = lax.broadcasted_iota(jnp.int32, (CX + 16, LANES), 1)
    first_x, last_x = gx == 0, gx == GX - 1
    row_from = jnp.where(first_x, 8, 0)
    row_to = jnp.where(last_x, 8 + CX, 16 + CX)
    inside_x = (row >= row_from) & (row < row_to)
    tile_from = jnp.where(gy == 0, 2, 0)
    tile_to = jnp.where(gy == GY - 1, TILES + 2, TILES + 4)
    z = lax.rem(lane_c, HALF)
    low_c = lane_c < HALF

    def couplings(t, carry):
        def load(place):
            row_end = jnp.where((place >= tile_from) & (place < tile_to), row_to, 0)
            return jnp.where(inside_x & (row < row_end), cond_ext[:, tile(place)], 0.0)

        here = load(t + 1)
        below, above = load(t), load(t + 2)
        swapped = swap_halves(here)
        outer = jnp.where(low_c, swap_halves(below), swap_halves(above))
        z_down = jnp.where(z == 0, 0.0, pltpu.roll(here, 1, 1))
        z_up = jnp.where(z == HALF - 1, 0.0, pltpu.roll(here, LANES - 1, 1))
        x_down = pltpu.roll(here, 1, 0)
        x_up = pltpu.roll(here, CX + 15, 0)
        total = 6.0 * here
        for k, there in enumerate((x_down, x_up, swapped, outer, z_down, z_up)):
            total = total + there
            face = jnp.where((here > 0.0) & (there > 0.0), -0.5 * (here + there), 0.0)
            coef[t, pl.ds(k, CX + 16, stride=8), :] = face
        coef[t, pl.ds(6, CX + 16, stride=8), :] = jnp.where(here > 0.0, 0.5 * total, 0.0)
        return carry

    lax.fori_loop(0, EXT_T, couplings, 0)

    for copy in copies + thirds:
        copy.wait_recv()

    def stencil(read, x, tiles, left, right, shift, emit):
        base = pl.multiple_of((x + 8 - REACH) * 8, 8)
        before = left
        value = read(x, tiles[0])
        turned = swap_halves(value)
        if before is None:
            before = turned
        for t in tiles:
            c = [
                jnp.broadcast_to(coef[t, pl.ds(base + k, 1), :], (SRC, LANES)) for k in range(7)
            ]
            if t == tiles[-1]:
                following, after = None, turned if right is None else right
            else:
                following = read(x, t + 1)
                after = swap_halves(following)
            diagonal = c[6] if shift == 0.0 else c[6] - shift
            total = diagonal * value
            total = total + c[0] * read(x - 1, t)
            total = total + c[1] * read(x + 1, t)
            total = total + c[2] * turned
            total = total + c[3] * jnp.where(low, before, after)
            total = total + c[4] * pltpu.roll(value, 1, 1)
            total = total + c[5] * pltpu.roll(value, LANES - 1, 1)
            emit(t, total)
            value, before, turned = following, turned, after

    spot = jnp.zeros((SRC, LANES), jnp.int32)
    source = lax.broadcasted_iota(jnp.int32, (SRC, LANES), 0)
    for k in range(SRC):
        spot = jnp.where(source == k, electrodes[k], spot)
    spot = spot - lane

    def first_row(x, carry):
        cell_x = gx * CX + x - REACH
        inside = (cell_x >= 0) & (cell_x < GX * CX)
        origin = (cell_x * (GY * TILES) + gy * TILES - 1) * LANES
        p = x - REACH
        centre = (p >= 0) & (p < CX)
        held = jnp.where(centre, lax.rem(p + CX // 2, CX // 2), 0)
        far = p >= CX // 2
        left = third_in[0, held]
        right = third_in[1, held]
        left = jnp.where(far, swap_halves(left), left)
        right = jnp.where(far, swap_halves(right), right)

        def emit(t, total):
            ok = inside
            if t == 0:
                ok = ok & (gy > 0)
            if t == EXT_T - 1:
                ok = ok & (gy < GY - 1)
            cell = jnp.where(ok, origin + t * LANES, -(2**30))
            field[x, pl.ds(0, SRC), tile(t)] = jnp.where(spot == cell, 20.0, 0.0) - total

        stencil(
            lambda i, t: start[i, :, tile(t)], x, range(EXT_T), left, right, 0.0, emit
        )
        return carry

    lax.fori_loop(1, EXT_X - 1, first_row, 0)

    def second_row(x, carry):
        def emit(t, total):
            field[x, pl.ds(SRC, SRC), tile(t)] = total

        stencil(
            lambda i, t: field[i, pl.ds(0, SRC), tile(t)], x, range(EXT_T), None, None, 0.8, emit
        )
        return carry

    lax.fori_loop(2, EXT_X - 2, second_row, 0)

    def third_row(x, carry):
        def read(i, t):
            return field[i, pl.ds(SRC, SRC), tile(t)]

        def emit(t, total):
            field[x, pl.ds(2 * SRC, SRC), tile(t)] = total

        left = swap_halves(read(x, 0))
        right = swap_halves(read(x, EXT_T - 1))
        stencil(read, x, range(1, TILES + 1), left, right, 1.6, emit)
        return carry

    lax.fori_loop(REACH, REACH + CX, third_row, 0)

    def products(x, total):
        values = field[x + REACH, :, pl.ds(LANES, MERGED)]
        coarse = values.astype(jnp.bfloat16)
        fine = (values - coarse.astype(f32)).astype(jnp.bfloat16)
        both = jnp.concatenate([coarse, fine], axis=0)
        split[x] = both
        return total + lax.dot_general(
            both, both, (((1,), (1,)), ((), ())), preferred_element_type=f32
        )

    total = lax.fori_loop(0, CX, products, jnp.zeros((2 * COLS, 2 * COLS), f32))
    store = pltpu.make_async_copy(split, cols, local_sem.at[2])
    store.start()
    total = total[:COLS] + total[COLS:]
    total = total[:, :COLS] + total[:, COLS:]
    empty = jnp.zeros((COLS // 2, HALF - COLS), f32)
    total = jnp.concatenate([total[: COLS // 2], empty, total[COLS // 2 :], empty], axis=1)

    for kind, (size, part) in enumerate(zip(GROUPS, (part0, part1, part2))):
        me = place(kind, gx, gy)
        part[me] = total
        sums = []
        for step in range(1, size):
            copy = pltpu.make_async_remote_copy(
                src_ref=part.at[me],
                dst_ref=part.at[me],
                send_sem=sum_send.at[kind, step],
                recv_sem=sum_recv.at[kind, size - step],
                device_id=partner(kind, gx, gy, step),
                device_id_type=MESH,
            )
            copy.start()
            sums.append(copy)
        for copy in sums:
            copy.wait()
        total = part[0]
        for i in range(1, size):
            total = total + part[i]
    gram[...] = total

    for copy in cond_copies + copies + thirds:
        copy.wait_send()
    store.wait()


def basis_kernel(cols, gram, basis, triangle, held, result, load_sem, store_sem):
    f32 = jnp.float32
    chunks = 8
    width = MERGED // chunks
    loads = [
        pltpu.make_async_copy(
            cols.at[:, :, pl.ds(i * width, width)],
            held.at[:, :, pl.ds(i * width, width)],
            load_sem.at[i],
        )
        for i in range(chunks)
    ]
    for load in loads:
        load.start()

    packed = gram[...]
    full = jnp.concatenate([packed, pltpu.roll(packed, HALF, 1)], axis=0)
    row = lax.broadcasted_iota(jnp.int32, (COLS, LANES), 0)
    lane = lax.broadcasted_iota(jnp.int32, (COLS, LANES), 1)
    matrix = jnp.where(lane < COLS, full, jnp.where(lane == row + HALF, 1.0, 0.0))
    pivots = jnp.ones((COLS, LANES), f32)
    for k in range(COLS):
        pivot_row = matrix[k : k + 1, :]
        pivot = pivot_row[:, k : k + 1]
        column = matrix[:, k : k + 1]
        pivots = jnp.where(row == k, pivot, pivots)
        if k < COLS - 1:
            factor = jnp.where(row > k, column * (1.0 / pivot), 0.0)
            matrix = matrix - factor * pivot_row
    matrix = matrix * lax.rsqrt(pivots)
    size = math.sqrt(GX * CX * GY * MERGED)
    upper = jnp.where((lane >= row) & (lane < COLS), matrix * (1.0 / size), 0.0)
    triangle[...] = upper[:, :COLS]
    inverse = pltpu.roll(matrix, HALF, 1)[:, :COLS] * size
    coarse = inverse.astype(jnp.bfloat16)
    fine = (inverse - coarse.astype(f32)).astype(jnp.bfloat16)
    weights = jnp.concatenate([coarse, coarse, fine], axis=1)

    stores = []
    for i in range(chunks):
        loads[i].wait()

        def one(x, carry):
            both = held[x, :, pl.ds(i * width, width)]
            stack = jnp.concatenate([both, both[:COLS]], axis=0)
            solved = jnp.dot(weights, stack, preferred_element_type=f32)
            for t in range(width // LANES):
                result[i * (width // LANES) + t, pl.ds(x, COLS, stride=CX), :] = solved[
                    :, t * LANES : (t + 1) * LANES
                ]
            return carry

        lax.fori_loop(0, CX, one, 0, unroll=True)
        for t in range(i * (width // LANES), (i + 1) * (width // LANES)):
            store = pltpu.make_async_copy(
                result.at[t], basis.at[:, tile(t)], store_sem.at[t]
            )
            store.start()
            stores.append(store)
    for store in stores:
        store.wait()


def per_device(initial_guess, conductivity, electrodes):
    f32 = jnp.float32
    any_space = pl.BlockSpec(memory_space=pltpu.HBM)
    vmem = pl.BlockSpec(memory_space=pltpu.VMEM)
    smem = pl.BlockSpec(memory_space=pltpu.SMEM)
    dma = pltpu.SemaphoreType.DMA
    cols, gram = pl.pallas_call(
        krylov_kernel,
        out_shape=(
            jax.ShapeDtypeStruct((CX, 2 * COLS, MERGED), jnp.bfloat16),
            jax.ShapeDtypeStruct((COLS // 2, LANES), f32),
        ),
        in_specs=[any_space, any_space, smem],
        out_specs=(any_space, vmem),
        scratch_shapes=[
            pltpu.VMEM((TILES, SRC * CX, LANES), f32),
            pltpu.VMEM((EXT_X, SRC, EXT), f32),
            pltpu.VMEM((EXT_X, COLS, EXT), f32),
            pltpu.VMEM((CX + 16, EXT + 2 * LANES), f32),
            pltpu.VMEM((EXT_T, (CX + 16) * 8, LANES), f32),
            pltpu.VMEM((2, CX // 2, SRC, LANES), f32),
            pltpu.VMEM((2, CX // 2, SRC, LANES), f32),
            pltpu.VMEM((CX, 2 * COLS, MERGED), jnp.bfloat16),
            pltpu.VMEM((GROUPS[0], COLS // 2, LANES), f32),
            pltpu.VMEM((GROUPS[1], COLS // 2, LANES), f32),
            pltpu.VMEM((GROUPS[2], COLS // 2, LANES), f32),
            dma((TILES,)),
            dma((3,)),
            dma((8,)),
            dma((8,)),
            dma((8,)),
            dma((8,)),
            dma((2,)),
            dma((2,)),
            dma((3, 8)),
            dma((3, 8)),
        ],
        compiler_params=pltpu.CompilerParams(
            collective_id=0, has_side_effects=True, vmem_limit_bytes=60 * 2**20
        ),
        name="krylov",
    )(initial_guess.reshape(SRC * CX, MERGED), conductivity, electrodes)
    basis, triangle = pl.pallas_call(
        basis_kernel,
        out_shape=(
            jax.ShapeDtypeStruct((COLS * CX, MERGED), f32),
            jax.ShapeDtypeStruct((COLS, COLS), f32),
        ),
        in_specs=[any_space, vmem],
        out_specs=(any_space, vmem),
        scratch_shapes=[
            pltpu.VMEM((CX, 2 * COLS, MERGED), jnp.bfloat16),
            pltpu.VMEM((TILES, COLS * CX, LANES), f32),
            dma((8,)),
            dma((TILES,)),
        ],
        compiler_params=pltpu.CompilerParams(vmem_limit_bytes=60 * 2**20),
        name="basis",
    )(cols, gram)
    return basis.reshape(COLS, CX, MERGED), triangle


def solution(mesh):
    return jax.shard_map(
        per_device,
        mesh=mesh,
        in_specs=(P(None, "gx", "gy"), P("gx", "gy"), P()),
        out_specs=(P(None, "gx", "gy"), P()),
        check_vma=False,
    )
```

time: 280 us -> 60.4 us (0.22)
  blocking collectives: 80.4 us -> 0 us
  Pallas kernels: 0 us -> 59.6 us
  local copies, waits for them, and re-layouts: 52.7 us -> 0 us
  other arithmetic: 51.2 us -> 0 us
  starting transfers between devices: 34.8 us -> 0 us
  waiting for transfers between devices: 34.7 us -> 0 us
  matrix products: 24.4 us -> 0 us
    psum x1 -> x0, blocking collectives: 80.4 us -> none  [per_device(): gram = lax.psum(local_gram, ('gx', 'gy'))]
    pallas_call x0 -> x2, Pallas kernels: none -> 59.6 us  [the longest x1 48.7 us: per_device(): pl.pallas_call(krylov_kernel, out_shape=(jax.ShapeDtypeStruct((CX, 2 * CO...]
    ppermute x12 -> x0, starting transfers between devices: 34.8 us -> none  [the longest x6 24.9 us: with_halo(): lax.ppermute(tail, axis, [(i, (i + 1) % count) for i in range(ends)])]
    ppermute x12 -> x0, waiting for transfers between devices: 34.7 us -> none  [the longest x6 26.6 us: with_halo(): lax.ppermute(head, axis, [((i + 1) % count, i) for i in range(ends)])]
    sub x3 -> x0, other arithmetic: 21.6 us -> none  [the longest x1 9.37 us: per_device(): first = source_field - apply_rimmed(field_one, cond_one)]
    concatenate x2 -> x0, local copies, waits for them, and re-layouts: 21 us -> none  [the longest x1 13.1 us: per_device(): jnp.concatenate([first, second, third], 0)]
    concatenate x6 -> x0, other arithmetic: 18.4 us -> none  [the longest x1 10.2 us: per_device(): jnp.concatenate([first, second, third], 0)]
    dot_general x1 -> x0, matrix products: 16.2 us -> none  [per_device(): local_gram = jnp.dot(columns, columns.T, precision=lax.Precision.HIGHEST)]
  transfers between devices with their start and end apart: 12 -> 0, of which waited for: 12 -> 0; matrix products, arithmetic and copies ran while one was open for 0% -> 0% of each run, Pallas kernels for 0% -> 0%
where the time goes in v1:
time: 60.4 us; the launch traced here: 60.2 us
  Pallas kernels  59.6 us (99%)
  between operations  0.64 us (1%)
    pallas_call x1, Pallas kernels, per_device(): pl.pallas_call(krylov_kernel, out_shape=(jax.ShapeDtypeStruct((CX, 2 * CO...  48.7 us
    pallas_call x1, Pallas kernels, per_device(): pl.pallas_call(basis_kernel, out_shape=(jax.ShapeDtypeStruct((COLS * CX,...  10.8 us

profile of v1, /device:TPU:1, one launch (start us, length us, event | category | flops | bytes accessed | tf_op | source)
XLA Modules:
  0.0 60.2 jit_solution(18039273106659370095)
XLA Ops:
  0.6 48.7 %krylov.1 = (bf16[16,96,2048]{2,1,0:T(8,128)(2,1)}, f32[24,128]{1,0:T(8,128)}) custom-call(f32[256,2048]{1,0:T(8,128)} %bitcast.2, f32[16,2048]{1,0:T(8,128)} %cond.1, s32[16]{0:T(128)} %electrodes.1), custom_call_target="tpu_custom_call" | custom-call | tf_op jit(solution)/shard_map/krylov/pallas_call | solution.py:448
  49.4 10.8 %basis.1 = (f32[768,2048]{1,0:T(8,128)}, f32[48,48]{1,0:T(8,128)}) custom-call(bf16[16,96,2048]{2,1,0:T(8,128)(2,1)} %get-tuple-element.6.cols, f32[24,128]{1,0:T(8,128)} %get-tuple-element.7.gram), custom_call_target="tpu_custom_call" | custom-call | tf_op jit(solution)/shard_map/basis/pallas_call | solution.py:484

commit v2 on v1

--- a/solution.py
+++ b/solution.py
@@ -60,6 +60,8 @@
     natural,
     start,
     field,
+    field_s,
+    field_t,
     cond_ext,
     coef,
     third_out,
@@ -87,7 +89,12 @@
         return (lax.rem(gx + dx + GX, GX), lax.rem(gy + dy + GY, GY))
 
     loads = [
-        pltpu.make_async_copy(guess.at[:, tile(t)], natural.at[t], guess_sem.at[t])
+        pltpu.make_async_copy(
+            guess.at[:, h, :, tile(t)],
+            natural.at[h, t].reshape(SRC, 8, LANES),
+            guess_sem.at[h, t],
+        )
+        for h in range(2)
         for t in range(TILES)
     ]
     for load in loads:
@@ -117,8 +124,9 @@
         load.wait()
 
     def lay_out(x, carry):
+        half, rest = x // 8, lax.rem(x, 8)
         for t in range(TILES):
-            start[x + REACH, :, tile(t + 1)] = natural[t, pl.ds(x, SRC, stride=CX), :]
+            start[x + REACH, :, tile(t + 1)] = natural[half, t, pl.ds(rest, SRC, stride=8), :]
         return carry
 
     lax.fori_loop(0, CX, lay_out, 0)
@@ -261,13 +269,10 @@
                 following = read(x, t + 1)
                 after = swap_halves(following)
             diagonal = c[6] if shift == 0.0 else c[6] - shift
-            total = diagonal * value
-            total = total + c[0] * read(x - 1, t)
-            total = total + c[1] * read(x + 1, t)
-            total = total + c[2] * turned
-            total = total + c[3] * jnp.where(low, before, after)
-            total = total + c[4] * pltpu.roll(value, 1, 1)
-            total = total + c[5] * pltpu.roll(value, LANES - 1, 1)
+            near = diagonal * value + c[2] * turned
+            across = c[0] * read(x - 1, t) + c[1] * read(x + 1, t)
+            along = c[4] * pltpu.roll(value, 1, 1) + c[5] * pltpu.roll(value, LANES - 1, 1)
+            total = (near + across) + (along + c[3] * jnp.where(low, before, after))
             emit(t, total)
             value, before, turned = following, turned, after
 
@@ -297,42 +302,42 @@
             if t == EXT_T - 1:
                 ok = ok & (gy < GY - 1)
             cell = jnp.where(ok, origin + t * LANES, -(2**30))
-            field[x, pl.ds(0, SRC), tile(t)] = jnp.where(spot == cell, 20.0, 0.0) - total
+            field[x, :, tile(t)] = jnp.where(spot == cell, 20.0, 0.0) - total
 
         stencil(
             lambda i, t: start[i, :, tile(t)], x, range(EXT_T), left, right, 0.0, emit
         )
         return carry
 
-    lax.fori_loop(1, EXT_X - 1, first_row, 0)
 
     def second_row(x, carry):
         def emit(t, total):
-            field[x, pl.ds(SRC, SRC), tile(t)] = total
+            field_s[x, :, tile(t)] = total
 
         stencil(
-            lambda i, t: field[i, pl.ds(0, SRC), tile(t)], x, range(EXT_T), None, None, 0.8, emit
-        )
-        return carry
-
-    lax.fori_loop(2, EXT_X - 2, second_row, 0)
+            lambda i, t: field[i, :, tile(t)], x, range(EXT_T), None, None, 0.8, emit
+        )
+        return carry
+
 
     def third_row(x, carry):
         def read(i, t):
-            return field[i, pl.ds(SRC, SRC), tile(t)]
+            return field_s[i, :, tile(t)]
 
         def emit(t, total):
-            field[x, pl.ds(2 * SRC, SRC), tile(t)] = total
+            field_t[x - REACH, :, tile(t)] = total
 
         left = swap_halves(read(x, 0))
         right = swap_halves(read(x, EXT_T - 1))
         stencil(read, x, range(1, TILES + 1), left, right, 1.6, emit)
         return carry
 
-    lax.fori_loop(REACH, REACH + CX, third_row, 0)
 
     def products(x, total):
-        values = field[x + REACH, :, pl.ds(LANES, MERGED)]
+        inner = pl.ds(LANES, MERGED)
+        values = jnp.concatenate(
+            [field[x + REACH, :, inner], field_s[x + REACH, :, inner], field_t[x, :, inner]], axis=0
+        )
         coarse = values.astype(jnp.bfloat16)
         fine = (values - coarse.astype(f32)).astype(jnp.bfloat16)
         both = jnp.concatenate([coarse, fine], axis=0)
@@ -341,7 +346,29 @@
             both, both, (((1,), (1,)), ((), ())), preferred_element_type=f32
         )
 
-    total = lax.fori_loop(0, CX, products, jnp.zeros((2 * COLS, 2 * COLS), f32))
+    def sweep(begin, end, stages, total):
+        def step(x, total):
+            if "products" in stages:
+                total = products(x - 5 - REACH, total)
+            if "third" in stages:
+                third_row(x - 4, 0)
+            if "second" in stages:
+                second_row(x - 2, 0)
+            if "first" in stages:
+                first_row(x, 0)
+            return total
+
+        return lax.fori_loop(begin, end, step, total)
+
+    total = jnp.zeros((2 * COLS, 2 * COLS), f32)
+    last = EXT_X - 1
+    sweep(1, 4, ("first",), 0)
+    sweep(4, 7, ("first", "second"), 0)
+    sweep(7, 8, ("first", "second", "third"), 0)
+    total = sweep(8, last, ("first", "second", "third", "products"), total)
+    total = sweep(last, last + 1, ("second", "third", "products"), total)
+    total = sweep(last + 1, last + 2, ("third", "products"), total)
+    total = sweep(last + 2, last + 3, ("products",), total)
     store = pltpu.make_async_copy(split, cols, local_sem.at[2])
     store.start()
     total = total[:COLS] + total[COLS:]
@@ -380,33 +407,58 @@
     f32 = jnp.float32
     chunks = 8
     width = MERGED // chunks
-    loads = [
-        pltpu.make_async_copy(
-            cols.at[:, :, pl.ds(i * width, width)],
-            held.at[:, :, pl.ds(i * width, width)],
-            load_sem.at[i],
-        )
-        for i in range(chunks)
-    ]
-    for load in loads:
-        load.start()
+
+    def part(i):
+        lanes = pl.ds(pl.multiple_of(i * width, width), width)
+        return pltpu.make_async_copy(cols.at[:, :, lanes], held.at[:, :, lanes], load_sem.at[i])
+
+    def begin(i, carry):
+        part(i).start()
+        return carry
+
+    lax.fori_loop(0, chunks, begin, 0)
 
     packed = gram[...]
     full = jnp.concatenate([packed, pltpu.roll(packed, HALF, 1)], axis=0)
+    row = lax.broadcasted_iota(jnp.int32, (8, LANES), 0)
+    lane = lax.broadcasted_iota(jnp.int32, (8, LANES), 1)
+    count = COLS // 8
+    matrix = []
+    for i in range(count):
+        unit = jnp.where(lane == row + (HALF + 8 * i), 1.0, 0.0)
+        matrix.append(jnp.where(lane < COLS, full[8 * i : 8 * i + 8], unit))
+    pivots = [jnp.ones((8, LANES), f32) for _ in range(count)]
+
+    def across(v, k):
+        return jnp.broadcast_to(v[:, k : k + 1], (8, LANES))
+
+    def down(v, r):
+        return jnp.broadcast_to(v[r : r + 1, :], (8, LANES))
+
+    for k in range(0, COLS, 2):
+        block, r = k // 8, k % 8
+        near = {i: across(matrix[i], k) for i in range(block, count)}
+        far = {i: across(matrix[i], k + 1) for i in range(block, count)}
+        row_near = down(matrix[block], r)
+        row_far = down(matrix[block], r + 1)
+        p, q, o = down(near[block], r), down(far[block], r + 1), down(far[block], r)
+        inverse_near = 1.0 / p
+        inverse_far = p / (p * q - o * o)
+        ratio = o * inverse_near
+        row_far = row_far - ratio * row_near
+        for i in range(block, count):
+            first = near[i] * inverse_near
+            second = (far[i] - first * o) * inverse_far
+            if i == block:
+                second = jnp.where(row > r + 1, second, 0.0)
+                pivots[i] = jnp.where(row == r, p, pivots[i])
+                pivots[i] = jnp.where(row == r + 1, q - ratio * o, pivots[i])
+                first = jnp.where(row > r, first, 0.0)
+            matrix[i] = matrix[i] - (first * row_near + second * row_far)
+    size = math.sqrt(GX * CX * GY * MERGED)
+    matrix = jnp.concatenate([m * lax.rsqrt(p) for m, p in zip(matrix, pivots)], axis=0)
     row = lax.broadcasted_iota(jnp.int32, (COLS, LANES), 0)
     lane = lax.broadcasted_iota(jnp.int32, (COLS, LANES), 1)
-    matrix = jnp.where(lane < COLS, full, jnp.where(lane == row + HALF, 1.0, 0.0))
-    pivots = jnp.ones((COLS, LANES), f32)
-    for k in range(COLS):
-        pivot_row = matrix[k : k + 1, :]
-        pivot = pivot_row[:, k : k + 1]
-        column = matrix[:, k : k + 1]
-        pivots = jnp.where(row == k, pivot, pivots)
-        if k < COLS - 1:
-            factor = jnp.where(row > k, column * (1.0 / pivot), 0.0)
-            matrix = matrix - factor * pivot_row
-    matrix = matrix * lax.rsqrt(pivots)
-    size = math.sqrt(GX * CX * GY * MERGED)
     upper = jnp.where((lane >= row) & (lane < COLS), matrix * (1.0 / size), 0.0)
     triangle[...] = upper[:, :COLS]
     inverse = pltpu.roll(matrix, HALF, 1)[:, :COLS] * size
@@ -414,29 +466,37 @@
     fine = (inverse - coarse.astype(f32)).astype(jnp.bfloat16)
     weights = jnp.concatenate([coarse, coarse, fine], axis=1)
 
-    stores = []
-    for i in range(chunks):
-        loads[i].wait()
-
-        def one(x, carry):
-            both = held[x, :, pl.ds(i * width, width)]
+    per_chunk = width // LANES
+
+    def send(h, t):
+        return pltpu.make_async_copy(
+            result.at[h, t].reshape(COLS, 8, LANES), basis.at[:, h, :, tile(t)], store_sem.at[h, t]
+        )
+
+    def solve(i, carry):
+        part(i).wait()
+        lanes = pl.ds(pl.multiple_of(i * width, width), width)
+        for x in range(CX):
+            both = held[x, :, lanes]
             stack = jnp.concatenate([both, both[:COLS]], axis=0)
             solved = jnp.dot(weights, stack, preferred_element_type=f32)
-            for t in range(width // LANES):
-                result[i * (width // LANES) + t, pl.ds(x, COLS, stride=CX), :] = solved[
+            for t in range(per_chunk):
+                result[x // 8, i * per_chunk + t, pl.ds(x % 8, COLS, stride=8), :] = solved[
                     :, t * LANES : (t + 1) * LANES
                 ]
-            return carry
-
-        lax.fori_loop(0, CX, one, 0, unroll=True)
-        for t in range(i * (width // LANES), (i + 1) * (width // LANES)):
-            store = pltpu.make_async_copy(
-                result.at[t], basis.at[:, tile(t)], store_sem.at[t]
-            )
-            store.start()
-            stores.append(store)
-    for store in stores:
-        store.wait()
+        for h in range(2):
+            for t in range(per_chunk):
+                send(h, i * per_chunk + t).start()
+        return carry
+
+    lax.fori_loop(0, chunks, solve, 0)
+
+    def finish(t, carry):
+        for h in range(2):
+            send(h, t).wait()
+        return carry
+
+    lax.fori_loop(0, TILES, finish, 0)
 
 
 def per_device(initial_guess, conductivity, electrodes):
@@ -454,9 +514,11 @@
         in_specs=[any_space, any_space, smem],
         out_specs=(any_space, vmem),
         scratch_shapes=[
-            pltpu.VMEM((TILES, SRC * CX, LANES), f32),
+            pltpu.VMEM((2, TILES, SRC * 8, LANES), f32),
             pltpu.VMEM((EXT_X, SRC, EXT), f32),
-            pltpu.VMEM((EXT_X, COLS, EXT), f32),
+            pltpu.VMEM((EXT_X, SRC, EXT), f32),
+            pltpu.VMEM((EXT_X, SRC, EXT), f32),
+            pltpu.VMEM((CX, SRC, EXT), f32),
             pltpu.VMEM((CX + 16, EXT + 2 * LANES), f32),
             pltpu.VMEM((EXT_T, (CX + 16) * 8, LANES), f32),
             pltpu.VMEM((2, CX // 2, SRC, LANES), f32),
@@ -465,7 +527,7 @@
             pltpu.VMEM((GROUPS[0], COLS // 2, LANES), f32),
             pltpu.VMEM((GROUPS[1], COLS // 2, LANES), f32),
             pltpu.VMEM((GROUPS[2], COLS // 2, LANES), f32),
-            dma((TILES,)),
+            dma((2, TILES)),
             dma((3,)),
             dma((8,)),
             dma((8,)),
@@ -480,20 +542,20 @@
             collective_id=0, has_side_effects=True, vmem_limit_bytes=60 * 2**20
         ),
         name="krylov",
-    )(initial_guess.reshape(SRC * CX, MERGED), conductivity, electrodes)
+    )(initial_guess.reshape(SRC, 2, 8, MERGED), conductivity, electrodes)
     basis, triangle = pl.pallas_call(
         basis_kernel,
         out_shape=(
-            jax.ShapeDtypeStruct((COLS * CX, MERGED), f32),
+            jax.ShapeDtypeStruct((COLS, 2, 8, MERGED), f32),
             jax.ShapeDtypeStruct((COLS, COLS), f32),
         ),
         in_specs=[any_space, vmem],
         out_specs=(any_space, vmem),
         scratch_shapes=[
             pltpu.VMEM((CX, 2 * COLS, MERGED), jnp.bfloat16),
-            pltpu.VMEM((TILES, COLS * CX, LANES), f32),
+            pltpu.VMEM((2, TILES, COLS * 8, LANES), f32),
             dma((8,)),
-            dma((TILES,)),
+            dma((2, TILES)),
         ],
         compiler_params=pltpu.CompilerParams(vmem_limit_bytes=60 * 2**20),
         name="basis",

time: 60.4 us -> 50.4 us (0.83)
  Pallas kernels: 59.6 us -> 49.4 us
    pallas_call x1, Pallas kernels: 48.7 us -> 41 us  [per_device(): pl.pallas_call(krylov_kernel, out_shape=(jax.ShapeDtypeStruct((CX, 2 * CO...]
    pallas_call x1, Pallas kernels: 10.8 us -> 8.35 us  [per_device(): pl.pallas_call(basis_kernel, out_shape=(jax.ShapeDtypeStruct((COLS, 2, 8,...]
where the time goes in v2:
time: 50.4 us; the launch traced here: 50 us
  Pallas kernels  49.4 us (98%)
  between operations  0.64 us (1%)
    pallas_call x1, Pallas kernels, per_device(): pl.pallas_call(krylov_kernel, out_shape=(jax.ShapeDtypeStruct((CX, 2 * CO...  41 us
    pallas_call x1, Pallas kernels, per_device(): pl.pallas_call(basis_kernel, out_shape=(jax.ShapeDtypeStruct((COLS, 2, 8,...  8.35 us

profile of v2, /device:TPU:1, one launch (start us, length us, event | category | flops | bytes accessed | tf_op | source)
XLA Modules:
  0.0 50.0 jit_solution(17440000647877371817)
XLA Ops:
  0.6 41.0 %krylov.1 = (bf16[16,96,2048]{2,1,0:T(8,128)(2,1)}, f32[24,128]{1,0:T(8,128)}) custom-call(f32[16,2,8,2048]{3,2,1,0:T(8,128)} %bitcast.2, f32[16,2048]{1,0:T(8,128)} %cond.1, s32[16]{0:T(128)} %electrodes.1), custom_call_target="tpu_custom_call" | custom-call | tf_op jit(solution)/shard_map/krylov/pallas_call | solution.py:508
  41.7 8.3 %basis.1 = (f32[48,2,8,2048]{3,2,1,0:T(8,128)}, f32[48,48]{1,0:T(8,128)}) custom-call(bf16[16,96,2048]{2,1,0:T(8,128)(2,1)} %get-tuple-element.6.cols, f32[24,128]{1,0:T(8,128)} %get-tuple-element.7.gram), custom_call_target="tpu_custom_call" | custom-call | tf_op jit(solution)/shard_map/basis/pallas_call | solution.py:546

commit v3 on v2

--- a/solution.py
+++ b/solution.py
@@ -64,6 +64,8 @@
     field_t,
     cond_ext,
     coef,
+    cond_out,
+    cond_in,
     third_out,
     third_in,
     split,
@@ -88,25 +90,30 @@
         dx, dy = move
         return (lax.rem(gx + dx + GX, GX), lax.rem(gy + dy + GY, GY))
 
-    loads = [
-        pltpu.make_async_copy(
-            guess.at[:, h, :, tile(t)],
-            natural.at[h, t].reshape(SRC, 8, LANES),
-            guess_sem.at[h, t],
-        )
-        for h in range(2)
-        for t in range(TILES)
-    ]
-    for load in loads:
-        load.start()
+    barrier = pltpu.get_barrier_semaphore()
+    for move in MOVES:
+        pl.semaphore_signal(barrier, inc=1, device_id=beside(move), device_id_type=MESH)
+
+    def load(half, t):
+        return pltpu.make_async_copy(
+            guess.at[:, half, :, tile(t)],
+            natural.at[half, t].reshape(SRC, 8, LANES),
+            guess_sem.at[half, t],
+        )
+
+    def each_load(act):
+        def step(t, carry):
+            for half in range(2):
+                act(load(half, t))
+            return carry
+
+        lax.fori_loop(0, TILES, step, 0)
+
     load_cond = pltpu.make_async_copy(
         cond, cond_ext.at[pl.ds(8, CX), pl.ds(2 * LANES, MERGED)], local_sem.at[1]
     )
     load_cond.start()
-
-    barrier = pltpu.get_barrier_semaphore()
-    for move in MOVES:
-        pl.semaphore_signal(barrier, inc=1, device_id=beside(move), device_id_type=MESH)
+    each_load(lambda copy: copy.start())
     for kind, size in enumerate(GROUPS):
         for step in range(1, size):
             pl.semaphore_signal(
@@ -119,9 +126,12 @@
     for x in (0, 8 + CX):
         for t in (0, EXT_T + 1):
             cond_ext[pl.ds(x, 8), tile(t)] = jnp.zeros((8, LANES), f32)
-
-    for load in loads:
-        load.wait()
+        cond_ext[pl.ds(x, 8), pl.ds(2 * LANES, MERGED)] = jnp.zeros((8, MERGED), f32)
+    load_cond.wait()
+    for i, x in enumerate((8 + CX - 4, 8)):
+        cond_out[i] = cond_ext[pl.ds(x, 4), pl.ds(2 * LANES, MERGED)]
+
+    each_load(lambda copy: copy.wait())
 
     def lay_out(x, carry):
         half, rest = x // 8, lax.rem(x, 8)
@@ -129,45 +139,37 @@
             start[x + REACH, :, tile(t + 1)] = natural[half, t, pl.ds(rest, SRC, stride=8), :]
         return carry
 
-    lax.fori_loop(0, CX, lay_out, 0)
-
-    lane = lax.broadcasted_iota(jnp.int32, (SRC, LANES), 1)
-    low = lane < HALF
-
-    def pack_third(x, carry):
-        near, far = REACH + x, REACH + CX // 2 + x
-        third_out[0, x] = jnp.where(
-            low, swap_halves(start[near, :, tile(TILES - 1)]), start[far, :, tile(TILES - 1)]
-        )
-        third_out[1, x] = jnp.where(
-            low, start[far, :, tile(2)], swap_halves(start[near, :, tile(2)])
-        )
-        return carry
-
-    lax.fori_loop(0, CX // 2, pack_third, 0)
-
+    def lay_out_faces(x, carry):
+        lay_out(x, 0)
+        return lay_out(x + CX - REACH, carry)
+
+    lax.fori_loop(0, REACH, lay_out_faces, 0)
     pl.semaphore_wait(barrier, len(MOVES) + sum(GROUPS) - len(GROUPS))
 
     cond_copies = []
     for i, (dx, dy) in enumerate(MOVES):
         if dx == 0:
-            rows_from, rows_to, rows = pl.ds(0, CX), pl.ds(8, CX), CX
+            rows_from, rows_to = pl.ds(0, CX), pl.ds(8, CX)
         elif dx > 0:
             rows_from, rows_to = pl.ds(CX - 8, 8), pl.ds(0, 8)
         else:
             rows_from, rows_to = pl.ds(0, 8), pl.ds(8 + CX, 8)
         if dy == 0:
-            lanes_from, lanes_to = pl.ds(0, MERGED), pl.ds(2 * LANES, MERGED)
+            lanes_from = lanes_to = pl.ds(0, MERGED)
         elif dx == 0:
             lanes_from = pl.ds(MERGED - 2 * LANES if dy > 0 else 0, 2 * LANES)
             lanes_to = pl.ds(0 if dy > 0 else (TILES + 2) * LANES, 2 * LANES)
         else:
             lanes_from = tile(TILES - 1 if dy > 0 else 0)
             lanes_to = tile(1 if dy > 0 else TILES + 2)
+        source, target = cond.at[rows_from, lanes_from], cond_ext.at[rows_to, lanes_to]
+        if dy == 0:
+            side = 0 if dx > 0 else 1
+            source, target = cond_out.at[side], cond_in.at[side]
         cond_copies.append(
             pltpu.make_async_remote_copy(
-                src_ref=cond.at[rows_from, lanes_from],
-                dst_ref=cond_ext.at[rows_to, lanes_to],
+                src_ref=source,
+                dst_ref=target,
                 send_sem=cond_send.at[i],
                 recv_sem=cond_recv.at[i],
                 device_id=beside((dx, dy)),
@@ -209,12 +211,34 @@
         )
         for i, move in enumerate(((0, 1), (0, -1)))
     ]
-    for copy in cond_copies + copies + thirds:
+    along_x = [copy for copy, (dx, dy) in zip(copies, MOVES) if dx != 0]
+    along_y = [copy for copy, (dx, dy) in zip(copies, MOVES) if dx == 0]
+    for copy in cond_copies + along_x:
         copy.start()
 
-    load_cond.wait()
+    lax.fori_loop(REACH, CX - REACH, lay_out, 0)
+    lane = lax.broadcasted_iota(jnp.int32, (SRC, LANES), 1)
+    low = lane < HALF
+
+    def pack_third(x, carry):
+        near, far = REACH + x, REACH + CX // 2 + x
+        third_out[0, x] = jnp.where(
+            low, swap_halves(start[near, :, tile(TILES - 1)]), start[far, :, tile(TILES - 1)]
+        )
+        third_out[1, x] = jnp.where(
+            low, start[far, :, tile(2)], swap_halves(start[near, :, tile(2)])
+        )
+        return carry
+
+    lax.fori_loop(0, CX // 2, pack_third, 0)
+
+    for copy in along_y + thirds:
+        copy.start()
+
     for copy in cond_copies:
         copy.wait_recv()
+    for i, x in enumerate((4, 8 + CX)):
+        cond_ext[pl.ds(x, 4), pl.ds(2 * LANES, MERGED)] = cond_in[i]
     row = lax.broadcasted_iota(jnp.int32, (CX + 16, LANES), 0)
     lane_c = lax.broadcasted_iota(jnp.int32, (CX + 16, LANES), 1)
     first_x, last_x = gx == 0, gx == GX - 1
@@ -249,32 +273,31 @@
 
     lax.fori_loop(0, EXT_T, couplings, 0)
 
-    for copy in copies + thirds:
-        copy.wait_recv()
-
-    def stencil(read, x, tiles, left, right, shift, emit):
+    def stencil(read, x, runs, left, right, shift, emit):
         base = pl.multiple_of((x + 8 - REACH) * 8, 8)
-        before = left
-        value = read(x, tiles[0])
-        turned = swap_halves(value)
-        if before is None:
-            before = turned
-        for t in tiles:
-            c = [
-                jnp.broadcast_to(coef[t, pl.ds(base + k, 1), :], (SRC, LANES)) for k in range(7)
-            ]
-            if t == tiles[-1]:
-                following, after = None, turned if right is None else right
-            else:
-                following = read(x, t + 1)
-                after = swap_halves(following)
-            diagonal = c[6] if shift == 0.0 else c[6] - shift
-            near = diagonal * value + c[2] * turned
-            across = c[0] * read(x - 1, t) + c[1] * read(x + 1, t)
-            along = c[4] * pltpu.roll(value, 1, 1) + c[5] * pltpu.roll(value, LANES - 1, 1)
-            total = (near + across) + (along + c[3] * jnp.where(low, before, after))
-            emit(t, total)
-            value, before, turned = following, turned, after
+        for begin, end in runs:
+            value = read(x, begin)
+            turned = swap_halves(value)
+            before = left if begin == 0 else swap_halves(read(x, begin - 1))
+            if before is None:
+                before = turned
+            for t in range(begin, end):
+                c = [
+                    jnp.broadcast_to(coef[t, pl.ds(base + k, 1), :], (SRC, LANES))
+                    for k in range(7)
+                ]
+                if t == EXT_T - 1:
+                    following, after = None, turned if right is None else right
+                else:
+                    following = read(x, t + 1)
+                    after = swap_halves(following)
+                diagonal = c[6] if shift == 0.0 else c[6] - shift
+                near = diagonal * value + c[2] * turned
+                across = c[0] * read(x - 1, t) + c[1] * read(x + 1, t)
+                along = c[4] * pltpu.roll(value, 1, 1) + c[5] * pltpu.roll(value, LANES - 1, 1)
+                total = (near + across) + (along + c[3] * jnp.where(low, before, after))
+                emit(t, total)
+                value, before, turned = following, turned, after
 
     spot = jnp.zeros((SRC, LANES), jnp.int32)
     source = lax.broadcasted_iota(jnp.int32, (SRC, LANES), 0)
@@ -282,10 +305,7 @@
         spot = jnp.where(source == k, electrodes[k], spot)
     spot = spot - lane
 
-    def first_row(x, carry):
-        cell_x = gx * CX + x - REACH
-        inside = (cell_x >= 0) & (cell_x < GX * CX)
-        origin = (cell_x * (GY * TILES) + gy * TILES - 1) * LANES
+    def outer_thirds(x):
         p = x - REACH
         centre = (p >= 0) & (p < CX)
         held = jnp.where(centre, lax.rem(p + CX // 2, CX // 2), 0)
@@ -294,6 +314,15 @@
         right = third_in[1, held]
         left = jnp.where(far, swap_halves(left), left)
         right = jnp.where(far, swap_halves(right), right)
+        return left, right
+
+    def first_row(x, runs):
+        cell_x = gx * CX + x - REACH
+        inside = (cell_x >= 0) & (cell_x < GX * CX)
+        origin = (cell_x * (GY * TILES) + gy * TILES - 1) * LANES
+        left = right = None
+        if runs[0][0] == 0:
+            left, right = outer_thirds(x)
 
         def emit(t, total):
             ok = inside
@@ -304,71 +333,80 @@
             cell = jnp.where(ok, origin + t * LANES, -(2**30))
             field[x, :, tile(t)] = jnp.where(spot == cell, 20.0, 0.0) - total
 
-        stencil(
-            lambda i, t: start[i, :, tile(t)], x, range(EXT_T), left, right, 0.0, emit
-        )
-        return carry
-
-
-    def second_row(x, carry):
+        stencil(lambda i, t: start[i, :, tile(t)], x, runs, left, right, 0.0, emit)
+
+
+    def second_row(x, runs):
         def emit(t, total):
             field_s[x, :, tile(t)] = total
 
-        stencil(
-            lambda i, t: field[i, :, tile(t)], x, range(EXT_T), None, None, 0.8, emit
-        )
-        return carry
-
-
-    def third_row(x, carry):
+        stencil(lambda i, t: field[i, :, tile(t)], x, runs, None, None, 0.8, emit)
+
+    def third_row(x, runs):
         def read(i, t):
             return field_s[i, :, tile(t)]
 
         def emit(t, total):
             field_t[x - REACH, :, tile(t)] = total
 
-        left = swap_halves(read(x, 0))
-        right = swap_halves(read(x, EXT_T - 1))
-        stencil(read, x, range(1, TILES + 1), left, right, 1.6, emit)
-        return carry
-
-
-    def products(x, total):
-        inner = pl.ds(LANES, MERGED)
-        values = jnp.concatenate(
-            [field[x + REACH, :, inner], field_s[x + REACH, :, inner], field_t[x, :, inner]], axis=0
-        )
-        coarse = values.astype(jnp.bfloat16)
-        fine = (values - coarse.astype(f32)).astype(jnp.bfloat16)
-        both = jnp.concatenate([coarse, fine], axis=0)
-        split[x] = both
+        stencil(read, x, runs, None, None, 1.6, emit)
+
+    def products(x, runs, total):
+        pieces = []
+        for begin, end in runs:
+            inner = pl.ds(begin * LANES, (end - begin) * LANES)
+            values = jnp.concatenate(
+                [field[x, :, inner], field_s[x, :, inner], field_t[x - REACH, :, inner]], axis=0
+            )
+            coarse = values.astype(jnp.bfloat16)
+            fine = (values - coarse.astype(f32)).astype(jnp.bfloat16)
+            both = jnp.concatenate([coarse, fine], axis=0)
+            split[x - REACH, :, pl.ds((begin - 1) * LANES, (end - begin) * LANES)] = both
+            pieces.append(both)
+        both = pieces[0] if len(pieces) == 1 else jnp.concatenate(pieces, axis=1)
         return total + lax.dot_general(
             both, both, (((1,), (1,)), ((), ())), preferred_element_type=f32
         )
 
-    def sweep(begin, end, stages, total):
+    def sweep(begin, end, total, first=None, second=None, third=None, inner=None):
         def step(x, total):
-            if "products" in stages:
-                total = products(x - 5 - REACH, total)
-            if "third" in stages:
-                third_row(x - 4, 0)
-            if "second" in stages:
-                second_row(x - 2, 0)
-            if "first" in stages:
-                first_row(x, 0)
+            if inner:
+                total = products(x - 5, inner, total)
+            if third:
+                third_row(x - 4, third)
+            if second:
+                second_row(x - 2, second)
+            if first:
+                first_row(x, first)
             return total
 
         return lax.fori_loop(begin, end, step, total)
 
     total = jnp.zeros((2 * COLS, 2 * COLS), f32)
-    last = EXT_X - 1
-    sweep(1, 4, ("first",), 0)
-    sweep(4, 7, ("first", "second"), 0)
-    sweep(7, 8, ("first", "second", "third"), 0)
-    total = sweep(8, last, ("first", "second", "third", "products"), total)
-    total = sweep(last, last + 1, ("second", "third", "products"), total)
-    total = sweep(last + 1, last + 2, ("third", "products"), total)
-    total = sweep(last + 2, last + 3, ("products",), total)
+    f, s, t, p = ((2, 16),), ((3, 15),), ((4, 14),), ((4, 14),)
+    sweep(4, 7, 0, f)
+    sweep(7, 10, 0, f, s)
+    sweep(10, 11, 0, f, s, t)
+    total = sweep(11, 18, total, f, s, t, p)
+    total = sweep(18, 19, total, None, s, t, p)
+    total = sweep(19, 20, total, None, None, t, p)
+    total = sweep(20, 21, total, None, None, None, p)
+
+    for copy in copies + thirds:
+        copy.wait_recv()
+
+    f, s, t, p = ((0, 18),), ((0, 18),), ((1, 17),), ((1, 17),)
+    f_rim, s_rim = ((0, 2), (16, 18)), ((0, 3), (15, 18))
+    t_rim = p_rim = ((1, 4), (14, 17))
+    sweep(1, 4, 0, f)
+    sweep(4, 7, 0, f_rim, s)
+    sweep(7, 8, 0, f_rim, s_rim, t)
+    total = sweep(8, 11, total, f_rim, s_rim, t, p)
+    total = sweep(11, 18, total, f_rim, s_rim, t_rim, p_rim)
+    total = sweep(18, 21, total, f, s, t, p_rim)
+    total = sweep(21, 22, total, None, s, t, p)
+    total = sweep(22, 23, total, None, None, t, p)
+    total = sweep(23, 24, total, None, None, None, p)
     store = pltpu.make_async_copy(split, cols, local_sem.at[2])
     store.start()
     total = total[:COLS] + total[COLS:]
@@ -521,6 +559,8 @@
             pltpu.VMEM((CX, SRC, EXT), f32),
             pltpu.VMEM((CX + 16, EXT + 2 * LANES), f32),
             pltpu.VMEM((EXT_T, (CX + 16) * 8, LANES), f32),
+            pltpu.VMEM((2, 4, MERGED), f32),
+            pltpu.VMEM((2, 4, MERGED), f32),
             pltpu.VMEM((2, CX // 2, SRC, LANES), f32),
             pltpu.VMEM((2, CX // 2, SRC, LANES), f32),
             pltpu.VMEM((CX, 2 * COLS, MERGED), jnp.bfloat16),

time: 50.4 us -> 50.7 us (level)
  no operation moved by 1% of the time
where the time goes in v3:
time: 50.7 us; the launch traced here: 50.5 us
  Pallas kernels  49.9 us (98%)
  between operations  0.64 us (1%)
    pallas_call x1, Pallas kernels, per_device(): pl.pallas_call(krylov_kernel, out_shape=(jax.ShapeDtypeStruct((CX, 2 * CO...  41.5 us
    pallas_call x1, Pallas kernels, per_device(): pl.pallas_call(basis_kernel, out_shape=(jax.ShapeDtypeStruct((COLS, 2, 8,...  8.34 us

profile of v3, /device:TPU:1, one launch (start us, length us, event | category | flops | bytes accessed | tf_op | source)
XLA Modules:
  0.0 50.5 jit_solution(29067516182479285)
XLA Ops:
  0.6 41.5 %krylov.1 = (bf16[16,96,2048]{2,1,0:T(8,128)(2,1)}, f32[24,128]{1,0:T(8,128)}) custom-call(f32[16,2,8,2048]{3,2,1,0:T(8,128)} %bitcast.2, f32[16,2048]{1,0:T(8,128)} %cond.1, s32[16]{0:T(128)} %electrodes.1), custom_call_target="tpu_custom_call" | custom-call | tf_op jit(solution)/shard_map/krylov/pallas_call | solution.py:546
  42.2 8.3 %basis.1 = (f32[48,2,8,2048]{3,2,1,0:T(8,128)}, f32[48,48]{1,0:T(8,128)}) custom-call(bf16[16,96,2048]{2,1,0:T(8,128)(2,1)} %get-tuple-element.6.cols, f32[24,128]{1,0:T(8,128)} %get-tuple-element.7.gram), custom_call_target="tpu_custom_call" | custom-call | tf_op jit(solution)/shard_map/basis/pallas_call | solution.py:586

commit v4 on v3

--- a/solution.py
+++ b/solution.py
@@ -10,6 +10,7 @@
 
 MESH = pl.DeviceIdType.MESH
 NZ = 64
+SHARE = 2
 LANES = 128
 HALF = 64
 SRC = 16
@@ -64,6 +65,7 @@
     field_t,
     cond_ext,
     coef,
+    shifts,
     cond_out,
     cond_in,
     third_out,
@@ -131,19 +133,6 @@
     for i, x in enumerate((8 + CX - 4, 8)):
         cond_out[i] = cond_ext[pl.ds(x, 4), pl.ds(2 * LANES, MERGED)]
 
-    each_load(lambda copy: copy.wait())
-
-    def lay_out(x, carry):
-        half, rest = x // 8, lax.rem(x, 8)
-        for t in range(TILES):
-            start[x + REACH, :, tile(t + 1)] = natural[half, t, pl.ds(rest, SRC, stride=8), :]
-        return carry
-
-    def lay_out_faces(x, carry):
-        lay_out(x, 0)
-        return lay_out(x + CX - REACH, carry)
-
-    lax.fori_loop(0, REACH, lay_out_faces, 0)
     pl.semaphore_wait(barrier, len(MOVES) + sum(GROUPS) - len(GROUPS))
 
     cond_copies = []
@@ -176,6 +165,23 @@
                 device_id_type=MESH,
             )
         )
+    for copy in cond_copies:
+        copy.start()
+
+    each_load(lambda copy: copy.wait())
+
+    def lay_out(x, carry):
+        half, rest = x // 8, lax.rem(x, 8)
+        for t in range(TILES):
+            start[x + REACH, :, tile(t + 1)] = natural[half, t, pl.ds(rest, SRC, stride=8), :]
+        return carry
+
+    def lay_out_faces(x, carry):
+        lay_out(x, 0)
+        return lay_out(x + CX - REACH, carry)
+
+    lax.fori_loop(0, REACH, lay_out_faces, 0)
+
     copies = []
     for i, (dx, dy) in enumerate(MOVES):
         depth = REACH if dy == 0 else 2
@@ -213,7 +219,7 @@
     ]
     along_x = [copy for copy, (dx, dy) in zip(copies, MOVES) if dx != 0]
     along_y = [copy for copy, (dx, dy) in zip(copies, MOVES) if dx == 0]
-    for copy in cond_copies + along_x:
+    for copy in along_x:
         copy.start()
 
     lax.fori_loop(REACH, CX - REACH, lay_out, 0)
@@ -273,28 +279,69 @@
 
     lax.fori_loop(0, EXT_T, couplings, 0)
 
-    def stencil(read, x, runs, left, right, shift, emit):
+    inward = lax.rem(lax.broadcasted_iota(jnp.int32, (2 * LANES, 2 * LANES), 0), LANES)
+    outward = lax.broadcasted_iota(jnp.int32, (2 * LANES, 2 * LANES), 1)
+    outward = jnp.where(outward < LANES, outward - 1, outward - (LANES - 1))
+    shifts[...] = jnp.where(inward == outward, 1.0, 0.0).astype(jnp.bfloat16)
+
+    def along_z(values):
+        values = jnp.concatenate(values, axis=0)
+        coarse = values.astype(jnp.bfloat16)
+        fine = (values - coarse.astype(f32)).astype(jnp.bfloat16)
+        both = jnp.concatenate([coarse, fine], axis=1)
+        return jnp.dot(both, shifts[...], preferred_element_type=f32)
+
+    def around(read, jobs):
+        places = [
+            (x, t)
+            for x, runs in jobs
+            for begin, end in runs
+            for t in range(begin, end)
+            if t % SHARE == 1
+        ]
+        both = along_z([read(x, t) for x, t in places])
+        found = []
+        for x, runs in jobs:
+            row = {}
+            for begin, end in runs:
+                for t in range(begin, end):
+                    if t % SHARE == 1:
+                        row[t] = both[:SRC, :LANES], both[:SRC, LANES:]
+                        both = both[SRC:]
+            found.append(row)
+        return found
+
+    def stencil(read, x, runs, left, right, shift, emit, beside_z, closed=False):
         base = pl.multiple_of((x + 8 - REACH) * 8, 8)
         for begin, end in runs:
             value = read(x, begin)
             turned = swap_halves(value)
-            before = left if begin == 0 else swap_halves(read(x, begin - 1))
-            if before is None:
+            if closed:
                 before = turned
+            elif begin > 0:
+                before = swap_halves(read(x, begin - 1))
+            else:
+                before = turned if left is None else left
             for t in range(begin, end):
                 c = [
                     jnp.broadcast_to(coef[t, pl.ds(base + k, 1), :], (SRC, LANES))
                     for k in range(7)
                 ]
-                if t == EXT_T - 1:
+                if closed and t == end - 1:
+                    following, after = None, turned
+                elif t == EXT_T - 1:
                     following, after = None, turned if right is None else right
                 else:
                     following = read(x, t + 1)
                     after = swap_halves(following)
                 diagonal = c[6] if shift == 0.0 else c[6] - shift
+                if t in beside_z:
+                    z_down, z_up = beside_z[t]
+                else:
+                    z_down, z_up = pltpu.roll(value, 1, 1), pltpu.roll(value, LANES - 1, 1)
                 near = diagonal * value + c[2] * turned
                 across = c[0] * read(x - 1, t) + c[1] * read(x + 1, t)
-                along = c[4] * pltpu.roll(value, 1, 1) + c[5] * pltpu.roll(value, LANES - 1, 1)
+                along = c[4] * z_down + c[5] * z_up
                 total = (near + across) + (along + c[3] * jnp.where(low, before, after))
                 emit(t, total)
                 value, before, turned = following, turned, after
@@ -316,7 +363,14 @@
         right = jnp.where(far, swap_halves(right), right)
         return left, right
 
-    def first_row(x, runs):
+    def read_start(x, t):
+        return start[x, :, tile(t)]
+
+    def first_rows(jobs):
+        for (x, runs), beside_z in zip(jobs, around(read_start, jobs)):
+            first_row(x, runs, beside_z)
+
+    def first_row(x, runs, beside_z):
         cell_x = gx * CX + x - REACH
         inside = (cell_x >= 0) & (cell_x < GX * CX)
         origin = (cell_x * (GY * TILES) + gy * TILES - 1) * LANES
@@ -333,23 +387,35 @@
             cell = jnp.where(ok, origin + t * LANES, -(2**30))
             field[x, :, tile(t)] = jnp.where(spot == cell, 20.0, 0.0) - total
 
-        stencil(lambda i, t: start[i, :, tile(t)], x, runs, left, right, 0.0, emit)
-
-
-    def second_row(x, runs):
+        closed = runs[0][0] == 1
+        stencil(read_start, x, runs, left, right, 0.0, emit, beside_z, closed)
+
+
+    def read_first(x, t):
+        return field[x, :, tile(t)]
+
+    def second_rows(jobs):
+        for (x, runs), beside_z in zip(jobs, around(read_first, jobs)):
+            second_row(x, runs, beside_z)
+
+    def second_row(x, runs, beside_z):
         def emit(t, total):
             field_s[x, :, tile(t)] = total
 
-        stencil(lambda i, t: field[i, :, tile(t)], x, runs, None, None, 0.8, emit)
-
-    def third_row(x, runs):
-        def read(i, t):
-            return field_s[i, :, tile(t)]
-
+        stencil(read_first, x, runs, None, None, 0.8, emit, beside_z)
+
+    def read_second(x, t):
+        return field_s[x, :, tile(t)]
+
+    def third_rows(jobs):
+        for (x, runs), beside_z in zip(jobs, around(read_second, jobs)):
+            third_row(x, runs, beside_z)
+
+    def third_row(x, runs, beside_z):
         def emit(t, total):
             field_t[x - REACH, :, tile(t)] = total
 
-        stencil(read, x, runs, None, None, 1.6, emit)
+        stencil(read_second, x, runs, None, None, 1.6, emit, beside_z)
 
     def products(x, runs, total):
         pieces = []
@@ -365,7 +431,7 @@
             pieces.append(both)
         both = pieces[0] if len(pieces) == 1 else jnp.concatenate(pieces, axis=1)
         return total + lax.dot_general(
-            both, both, (((1,), (1,)), ((), ())), preferred_element_type=f32
+            both[:COLS], both, (((1,), (1,)), ((), ())), preferred_element_type=f32
         )
 
     def sweep(begin, end, total, first=None, second=None, third=None, inner=None):
@@ -373,17 +439,17 @@
             if inner:
                 total = products(x - 5, inner, total)
             if third:
-                third_row(x - 4, third)
+                third_rows([(x - 4, third)])
             if second:
-                second_row(x - 2, second)
+                second_rows([(x - 2, second)])
             if first:
-                first_row(x, first)
+                first_rows([(x, first)])
             return total
 
         return lax.fori_loop(begin, end, step, total)
 
-    total = jnp.zeros((2 * COLS, 2 * COLS), f32)
-    f, s, t, p = ((2, 16),), ((3, 15),), ((4, 14),), ((4, 14),)
+    total = jnp.zeros((COLS, 2 * COLS), f32)
+    f, s, t, p = ((1, 17),), ((2, 16),), ((3, 15),), ((3, 15),)
     sweep(4, 7, 0, f)
     sweep(7, 10, 0, f, s)
     sweep(10, 11, 0, f, s, t)
@@ -395,22 +461,45 @@
     for copy in copies + thirds:
         copy.wait_recv()
 
-    f, s, t, p = ((0, 18),), ((0, 18),), ((1, 17),), ((1, 17),)
-    f_rim, s_rim = ((0, 2), (16, 18)), ((0, 3), (15, 18))
-    t_rim = p_rim = ((1, 4), (14, 17))
-    sweep(1, 4, 0, f)
-    sweep(4, 7, 0, f_rim, s)
-    sweep(7, 8, 0, f_rim, s_rim, t)
-    total = sweep(8, 11, total, f_rim, s_rim, t, p)
-    total = sweep(11, 18, total, f_rim, s_rim, t_rim, p_rim)
-    total = sweep(18, 21, total, f, s, t, p_rim)
-    total = sweep(21, 22, total, None, s, t, p)
-    total = sweep(22, 23, total, None, None, t, p)
-    total = sweep(23, 24, total, None, None, None, p)
+    whole, rim = ((0, 18),), ((0, 2), (16, 18))
+    inner, inner_rim = ((1, 17),), ((1, 3), (15, 17))
+
+    def rest_of_first(i, carry):
+        rims = [(jnp.minimum(4 + 5 * i + j, CX + 1), rim) for j in range(5)]
+        first_rows([(1 + i, whole), (CX + 2 + i, whole), *rims])
+        return carry
+
+    def rest_of_second(i, carry):
+        rims = [(5 + 4 * i + j, rim) for j in range(4)]
+        second_rows([(2 + i, whole), (CX + 1 + i, whole), *rims])
+        return carry
+
+    def rest_of_third(i):
+        rims = [(jnp.minimum(6 + 4 * i + j, CX - 1), inner_rim) for j in range(4)]
+        third_rows([(3 + i, inner), (CX + i, inner), *rims])
+
+    def rest_of_products(i, total):
+        total = products(3 + i, inner, total)
+        total = products(CX + i, inner, total)
+        for j in range(3):
+            total = products(6 + 3 * i + j, inner_rim, total)
+        return total
+
+    def rest_of_both(i, total):
+        total = rest_of_products(i - 1, total)
+        rest_of_third(i)
+        return total
+
+    lax.fori_loop(0, REACH, rest_of_first, 0)
+    lax.fori_loop(0, REACH, rest_of_second, 0)
+    rest_of_third(0)
+    total = lax.fori_loop(1, REACH, rest_of_both, total)
+    total = rest_of_products(REACH - 1, total)
+    total = products(CX - 1, inner_rim, total)
     store = pltpu.make_async_copy(split, cols, local_sem.at[2])
     store.start()
-    total = total[:COLS] + total[COLS:]
-    total = total[:, :COLS] + total[:, COLS:]
+    mixed = total[:, COLS:]
+    total = total[:, :COLS] + (mixed + mixed.T)
     empty = jnp.zeros((COLS // 2, HALF - COLS), f32)
     total = jnp.concatenate([total[: COLS // 2], empty, total[COLS // 2 :], empty], axis=1)
 
@@ -559,6 +648,7 @@
             pltpu.VMEM((CX, SRC, EXT), f32),
             pltpu.VMEM((CX + 16, EXT + 2 * LANES), f32),
             pltpu.VMEM((EXT_T, (CX + 16) * 8, LANES), f32),
+            pltpu.VMEM((2 * LANES, 2 * LANES), jnp.bfloat16),
             pltpu.VMEM((2, 4, MERGED), f32),
             pltpu.VMEM((2, 4, MERGED), f32),
             pltpu.VMEM((2, CX // 2, SRC, LANES), f32),

time: 50.7 us -> 50.3 us (level)
  no operation moved by 1% of the time
where the time goes in v4:
time: 50.3 us; the launch traced here: 50.1 us
  Pallas kernels  49.5 us (98%)
  between operations  0.64 us (1%)
    pallas_call x1, Pallas kernels, per_device(): pl.pallas_call(krylov_kernel, out_shape=(jax.ShapeDtypeStruct((CX, 2 * CO...  41.1 us
    pallas_call x1, Pallas kernels, per_device(): pl.pallas_call(basis_kernel, out_shape=(jax.ShapeDtypeStruct((COLS, 2, 8,...  8.34 us

profile of v4, /device:TPU:1, one launch (start us, length us, event | category | flops | bytes accessed | tf_op | source)
XLA Modules:
  0.0 50.1 jit_solution(4398781324913952357)
XLA Ops:
  0.6 41.1 %krylov.1 = (bf16[16,96,2048]{2,1,0:T(8,128)(2,1)}, f32[24,128]{1,0:T(8,128)}) custom-call(f32[16,2,8,2048]{3,2,1,0:T(8,128)} %bitcast.2, f32[16,2048]{1,0:T(8,128)} %cond.1, s32[16]{0:T(128)} %electrodes.1), custom_call_target="tpu_custom_call" | custom-call | tf_op jit(solution)/shard_map/krylov/pallas_call | solution.py:635
  41.8 8.3 %basis.1 = (f32[48,2,8,2048]{3,2,1,0:T(8,128)}, f32[48,48]{1,0:T(8,128)}) custom-call(bf16[16,96,2048]{2,1,0:T(8,128)(2,1)} %get-tuple-element.6.cols, f32[24,128]{1,0:T(8,128)} %get-tuple-element.7.gram), custom_call_target="tpu_custom_call" | custom-call | tf_op jit(solution)/shard_map/basis/pallas_call | solution.py:676

commit v5 on v4

--- a/solution.py
+++ b/solution.py
@@ -19,6 +19,7 @@
 TILES = 16
 REACH = 3
 EXT_X = CX + 2 * REACH
+SPARE = EXT_X + 1
 EXT_T = TILES + 2
 EXT = EXT_T * LANES
 MERGED = TILES * LANES
@@ -93,8 +94,14 @@
         return (lax.rem(gx + dx + GX, GX), lax.rem(gy + dy + GY, GY))
 
     barrier = pltpu.get_barrier_semaphore()
-    for move in MOVES:
+
+    def greet(i, carry):
+        i = i + jnp.where(i >= 4, 1, 0)
+        move = (i // 3 - 1, lax.rem(i, 3) - 1)
         pl.semaphore_signal(barrier, inc=1, device_id=beside(move), device_id_type=MESH)
+        return carry
+
+    lax.fori_loop(0, len(MOVES), greet, 0)
 
     def load(half, t):
         return pltpu.make_async_copy(
@@ -117,11 +124,17 @@
     load_cond.start()
     each_load(lambda copy: copy.start())
     for kind, size in enumerate(GROUPS):
-        for step in range(1, size):
+
+
+        def greet_group(step, carry, kind=kind):
             pl.semaphore_signal(
                 barrier, inc=1, device_id=partner(kind, gx, gy, step), device_id_type=MESH
             )
-
+            return carry
+
+        lax.fori_loop(1, size, greet_group, 0)
+
+    third_in[:, CX // 2] = jnp.zeros((2, SRC, LANES), f32)
     for x in (0, EXT_X - 1):
         for t in (0, EXT_T - 1):
             start[x, :, tile(t)] = jnp.zeros((SRC, LANES), f32)
@@ -170,18 +183,6 @@
 
     each_load(lambda copy: copy.wait())
 
-    def lay_out(x, carry):
-        half, rest = x // 8, lax.rem(x, 8)
-        for t in range(TILES):
-            start[x + REACH, :, tile(t + 1)] = natural[half, t, pl.ds(rest, SRC, stride=8), :]
-        return carry
-
-    def lay_out_faces(x, carry):
-        lay_out(x, 0)
-        return lay_out(x + CX - REACH, carry)
-
-    lax.fori_loop(0, REACH, lay_out_faces, 0)
-
     copies = []
     for i, (dx, dy) in enumerate(MOVES):
         depth = REACH if dy == 0 else 2
@@ -209,7 +210,7 @@
     thirds = [
         pltpu.make_async_remote_copy(
             src_ref=third_out.at[i],
-            dst_ref=third_in.at[i],
+            dst_ref=third_in.at[i, pl.ds(0, CX // 2)],
             send_sem=third_send_sem.at[i],
             recv_sem=third_recv_sem.at[i],
             device_id=beside(move),
@@ -219,10 +220,20 @@
     ]
     along_x = [copy for copy, (dx, dy) in zip(copies, MOVES) if dx != 0]
     along_y = [copy for copy, (dx, dy) in zip(copies, MOVES) if dx == 0]
-    for copy in along_x:
-        copy.start()
-
-    lax.fori_loop(REACH, CX - REACH, lay_out, 0)
+
+    def lay_out(i, carry):
+        @pl.when(i == 2 * REACH)
+        def _():
+            for copy in along_x:
+                copy.start()
+
+        x = jnp.where(i < REACH, i, jnp.where(i < 2 * REACH, i + CX - 2 * REACH, i - REACH))
+        half, rest = x // 8, lax.rem(x, 8)
+        for t in range(TILES):
+            start[x + REACH, :, tile(t + 1)] = natural[half, t, pl.ds(rest, SRC, stride=8), :]
+        return carry
+
+    lax.fori_loop(0, CX, lay_out, 0)
     lane = lax.broadcasted_iota(jnp.int32, (SRC, LANES), 1)
     low = lane < HALF
 
@@ -242,7 +253,7 @@
         copy.start()
 
     for copy in cond_copies:
-        copy.wait_recv()
+        copy.wait()
     for i, x in enumerate((4, 8 + CX)):
         cond_ext[pl.ds(x, 4), pl.ds(2 * LANES, MERGED)] = cond_in[i]
     row = lax.broadcasted_iota(jnp.int32, (CX + 16, LANES), 0)
@@ -311,14 +322,12 @@
             found.append(row)
         return found
 
-    def stencil(read, x, runs, left, right, shift, emit, beside_z, closed=False):
+    def stencil(read, x, runs, left, right, shift, emit, beside_z):
         base = pl.multiple_of((x + 8 - REACH) * 8, 8)
         for begin, end in runs:
             value = read(x, begin)
             turned = swap_halves(value)
-            if closed:
-                before = turned
-            elif begin > 0:
+            if begin > 0:
                 before = swap_halves(read(x, begin - 1))
             else:
                 before = turned if left is None else left
@@ -327,9 +336,7 @@
                     jnp.broadcast_to(coef[t, pl.ds(base + k, 1), :], (SRC, LANES))
                     for k in range(7)
                 ]
-                if closed and t == end - 1:
-                    following, after = None, turned
-                elif t == EXT_T - 1:
+                if t == EXT_T - 1:
                     following, after = None, turned if right is None else right
                 else:
                     following = read(x, t + 1)
@@ -355,7 +362,7 @@
     def outer_thirds(x):
         p = x - REACH
         centre = (p >= 0) & (p < CX)
-        held = jnp.where(centre, lax.rem(p + CX // 2, CX // 2), 0)
+        held = jnp.where(centre, lax.rem(p + CX // 2, CX // 2), CX // 2)
         far = p >= CX // 2
         left = third_in[0, held]
         right = third_in[1, held]
@@ -387,8 +394,7 @@
             cell = jnp.where(ok, origin + t * LANES, -(2**30))
             field[x, :, tile(t)] = jnp.where(spot == cell, 20.0, 0.0) - total
 
-        closed = runs[0][0] == 1
-        stencil(read_start, x, runs, left, right, 0.0, emit, beside_z, closed)
+        stencil(read_start, x, runs, left, right, 0.0, emit, beside_z)
 
 
     def read_first(x, t):
@@ -417,7 +423,7 @@
 
         stencil(read_second, x, runs, None, None, 1.6, emit, beside_z)
 
-    def products(x, runs, total):
+    def products(x, runs):
         pieces = []
         for begin, end in runs:
             inner = pl.ds(begin * LANES, (end - begin) * LANES)
@@ -430,72 +436,29 @@
             split[x - REACH, :, pl.ds((begin - 1) * LANES, (end - begin) * LANES)] = both
             pieces.append(both)
         both = pieces[0] if len(pieces) == 1 else jnp.concatenate(pieces, axis=1)
-        return total + lax.dot_general(
+        return lax.dot_general(
             both[:COLS], both, (((1,), (1,)), ((), ())), preferred_element_type=f32
         )
 
-    def sweep(begin, end, total, first=None, second=None, third=None, inner=None):
-        def step(x, total):
-            if inner:
-                total = products(x - 5, inner, total)
-            if third:
-                third_rows([(x - 4, third)])
-            if second:
-                second_rows([(x - 2, second)])
-            if first:
-                first_rows([(x, first)])
-            return total
-
-        return lax.fori_loop(begin, end, step, total)
-
-    total = jnp.zeros((COLS, 2 * COLS), f32)
-    f, s, t, p = ((1, 17),), ((2, 16),), ((3, 15),), ((3, 15),)
-    sweep(4, 7, 0, f)
-    sweep(7, 10, 0, f, s)
-    sweep(10, 11, 0, f, s, t)
-    total = sweep(11, 18, total, f, s, t, p)
-    total = sweep(18, 19, total, None, s, t, p)
-    total = sweep(19, 20, total, None, None, t, p)
-    total = sweep(20, 21, total, None, None, None, p)
-
-    for copy in copies + thirds:
-        copy.wait_recv()
-
-    whole, rim = ((0, 18),), ((0, 2), (16, 18))
-    inner, inner_rim = ((1, 17),), ((1, 3), (15, 17))
-
-    def rest_of_first(i, carry):
-        rims = [(jnp.minimum(4 + 5 * i + j, CX + 1), rim) for j in range(5)]
-        first_rows([(1 + i, whole), (CX + 2 + i, whole), *rims])
-        return carry
-
-    def rest_of_second(i, carry):
-        rims = [(5 + 4 * i + j, rim) for j in range(4)]
-        second_rows([(2 + i, whole), (CX + 1 + i, whole), *rims])
-        return carry
-
-    def rest_of_third(i):
-        rims = [(jnp.minimum(6 + 4 * i + j, CX - 1), inner_rim) for j in range(4)]
-        third_rows([(3 + i, inner), (CX + i, inner), *rims])
-
-    def rest_of_products(i, total):
-        total = products(3 + i, inner, total)
-        total = products(CX + i, inner, total)
-        for j in range(3):
-            total = products(6 + 3 * i + j, inner_rim, total)
+    whole, inner = ((0, EXT_T),), ((1, TILES + 1),)
+
+    def turn(x, total):
+        @pl.when(x == 1)
+        def _():
+            for copy in copies + thirds:
+                copy.wait()
+
+        def row(shift, first, last):
+            return jnp.minimum(jnp.maximum(x - shift, first), last)
+
+        own = products(row(5, REACH, REACH + CX - 1), inner)
+        total = jnp.where(x >= 5 + REACH, total + own, 0.0)
+        third_rows([(row(4, REACH, REACH + CX - 1), inner)])
+        second_rows([(row(2, 2, EXT_X - 3), whole)])
+        first_rows([(jnp.where(x == 0, SPARE, row(0, 1, EXT_X - 2)), whole)])
         return total
 
-    def rest_of_both(i, total):
-        total = rest_of_products(i - 1, total)
-        rest_of_third(i)
-        return total
-
-    lax.fori_loop(0, REACH, rest_of_first, 0)
-    lax.fori_loop(0, REACH, rest_of_second, 0)
-    rest_of_third(0)
-    total = lax.fori_loop(1, REACH, rest_of_both, total)
-    total = rest_of_products(REACH - 1, total)
-    total = products(CX - 1, inner_rim, total)
+    total = lax.fori_loop(0, CX + 8, turn, jnp.zeros((COLS, 2 * COLS), f32))
     store = pltpu.make_async_copy(split, cols, local_sem.at[2])
     store.start()
     mixed = total[:, COLS:]
@@ -506,9 +469,9 @@
     for kind, (size, part) in enumerate(zip(GROUPS, (part0, part1, part2))):
         me = place(kind, gx, gy)
         part[me] = total
-        sums = []
-        for step in range(1, size):
-            copy = pltpu.make_async_remote_copy(
+
+        def share(step, kind=kind, size=size, part=part, me=me):
+            return pltpu.make_async_remote_copy(
                 src_ref=part.at[me],
                 dst_ref=part.at[me],
                 send_sem=sum_send.at[kind, step],
@@ -516,17 +479,22 @@
                 device_id=partner(kind, gx, gy, step),
                 device_id_type=MESH,
             )
-            copy.start()
-            sums.append(copy)
-        for copy in sums:
-            copy.wait()
+
+        def begin_share(step, carry, share=share):
+            share(step).start()
+            return carry
+
+        def end_share(step, carry, share=share):
+            share(step).wait()
+            return carry
+
+        lax.fori_loop(1, size, begin_share, 0)
+        lax.fori_loop(1, size, end_share, 0)
         total = part[0]
         for i in range(1, size):
             total = total + part[i]
     gram[...] = total
 
-    for copy in cond_copies + copies + thirds:
-        copy.wait_send()
     store.wait()
 
 
@@ -554,7 +522,6 @@
     for i in range(count):
         unit = jnp.where(lane == row + (HALF + 8 * i), 1.0, 0.0)
         matrix.append(jnp.where(lane < COLS, full[8 * i : 8 * i + 8], unit))
-    pivots = [jnp.ones((8, LANES), f32) for _ in range(count)]
 
     def across(v, k):
         return jnp.broadcast_to(v[:, k : k + 1], (8, LANES))
@@ -562,30 +529,37 @@
     def down(v, r):
         return jnp.broadcast_to(v[r : r + 1, :], (8, LANES))
 
-    for k in range(0, COLS, 2):
-        block, r = k // 8, k % 8
-        near = {i: across(matrix[i], k) for i in range(block, count)}
-        far = {i: across(matrix[i], k + 1) for i in range(block, count)}
-        row_near = down(matrix[block], r)
-        row_far = down(matrix[block], r + 1)
-        p, q, o = down(near[block], r), down(far[block], r + 1), down(far[block], r)
-        inverse_near = 1.0 / p
-        inverse_far = p / (p * q - o * o)
-        ratio = o * inverse_near
-        row_far = row_far - ratio * row_near
-        for i in range(block, count):
-            first = near[i] * inverse_near
-            second = (far[i] - first * o) * inverse_far
-            if i == block:
-                second = jnp.where(row > r + 1, second, 0.0)
-                pivots[i] = jnp.where(row == r, p, pivots[i])
-                pivots[i] = jnp.where(row == r + 1, q - ratio * o, pivots[i])
-                first = jnp.where(row > r, first, 0.0)
-            matrix[i] = matrix[i] - (first * row_near + second * row_far)
+    def eliminate(turn, carry):
+        matrix = list(carry)
+        for r in range(0, 8, 2):
+            near = [across(m, r) for m in matrix]
+            far = [across(m, r + 1) for m in matrix]
+            row_near = down(matrix[0], r)
+            row_far = down(matrix[0], r + 1)
+            p, q, o = down(near[0], r), down(far[0], r + 1), down(far[0], r)
+            inverse_near = 1.0 / p
+            inverse_far = p / (p * q - o * o)
+            ratio = o * inverse_near
+            row_far = row_far - ratio * row_near
+            for i in range(count):
+                first = near[i] * inverse_near
+                second = (far[i] - first * o) * inverse_far
+                if i == 0:
+                    first = jnp.where(row > r, first, 0.0)
+                    second = jnp.where(row > r + 1, second, 0.0)
+                change = first * row_near + second * row_far
+                if i > 0:
+                    change = jnp.where(turn < count - i, change, 0.0)
+                matrix[i] = matrix[i] - change
+        return tuple(pltpu.roll(m, LANES - 8, 1) for m in matrix[1:] + matrix[:1])
+
+    matrix = lax.fori_loop(0, count, eliminate, tuple(matrix))
     size = math.sqrt(GX * CX * GY * MERGED)
-    matrix = jnp.concatenate([m * lax.rsqrt(p) for m, p in zip(matrix, pivots)], axis=0)
+    matrix = pltpu.roll(jnp.concatenate(matrix, axis=0), COLS, 1)
     row = lax.broadcasted_iota(jnp.int32, (COLS, LANES), 0)
     lane = lax.broadcasted_iota(jnp.int32, (COLS, LANES), 1)
+    pivots = jnp.sum(jnp.where(lane == row, matrix, 0.0), axis=1, keepdims=True)
+    matrix = matrix * lax.rsqrt(pivots)
     upper = jnp.where((lane >= row) & (lane < COLS), matrix * (1.0 / size), 0.0)
     triangle[...] = upper[:, :COLS]
     inverse = pltpu.roll(matrix, HALF, 1)[:, :COLS] * size
@@ -603,18 +577,21 @@
     def solve(i, carry):
         part(i).wait()
         lanes = pl.ds(pl.multiple_of(i * width, width), width)
-        for x in range(CX):
-            both = held[x, :, lanes]
-            stack = jnp.concatenate([both, both[:COLS]], axis=0)
-            solved = jnp.dot(weights, stack, preferred_element_type=f32)
-            for t in range(per_chunk):
-                result[x // 8, i * per_chunk + t, pl.ds(x % 8, COLS, stride=8), :] = solved[
-                    :, t * LANES : (t + 1) * LANES
-                ]
-        for h in range(2):
+
+        def half(h, carry):
+            for rest in range(8):
+                both = held[h * 8 + rest, :, lanes]
+                stack = jnp.concatenate([both, both[:COLS]], axis=0)
+                solved = jnp.dot(weights, stack, preferred_element_type=f32)
+                for t in range(per_chunk):
+                    result[h, i * per_chunk + t, pl.ds(rest, COLS, stride=8), :] = solved[
+                        :, t * LANES : (t + 1) * LANES
+                    ]
             for t in range(per_chunk):
                 send(h, i * per_chunk + t).start()
-        return carry
+            return carry
+
+        return lax.fori_loop(0, 2, half, carry)
 
     lax.fori_loop(0, chunks, solve, 0)
 
@@ -642,9 +619,9 @@
         out_specs=(any_space, vmem),
         scratch_shapes=[
             pltpu.VMEM((2, TILES, SRC * 8, LANES), f32),
-            pltpu.VMEM((EXT_X, SRC, EXT), f32),
-            pltpu.VMEM((EXT_X, SRC, EXT), f32),
-            pltpu.VMEM((EXT_X, SRC, EXT), f32),
+            pltpu.VMEM((EXT_X + 3, SRC, EXT), f32),
+            pltpu.VMEM((EXT_X + 3, SRC, EXT), f32),
+            pltpu.VMEM((EXT_X + 3, SRC, EXT), f32),
             pltpu.VMEM((CX, SRC, EXT), f32),
             pltpu.VMEM((CX + 16, EXT + 2 * LANES), f32),
             pltpu.VMEM((EXT_T, (CX + 16) * 8, LANES), f32),
@@ -652,7 +629,7 @@
             pltpu.VMEM((2, 4, MERGED), f32),
             pltpu.VMEM((2, 4, MERGED), f32),
             pltpu.VMEM((2, CX // 2, SRC, LANES), f32),
-            pltpu.VMEM((2, CX // 2, SRC, LANES), f32),
+            pltpu.VMEM((2, CX // 2 + 1, SRC, LANES), f32),
             pltpu.VMEM((CX, 2 * COLS, MERGED), jnp.bfloat16),
             pltpu.VMEM((GROUPS[0], COLS // 2, LANES), f32),
             pltpu.VMEM((GROUPS[1], COLS // 2, LANES), f32),

time: 50.3 us -> 55.7 us (1.11)
  Pallas kernels: 49.5 us -> 54.8 us
    pallas_call x1, Pallas kernels: 41.1 us -> 44.9 us  [per_device(): pl.pallas_call(krylov_kernel, out_shape=(jax.ShapeDtypeStruct((CX, 2 * CO...]
    pallas_call x1, Pallas kernels: 8.34 us -> 9.96 us  [per_device(): pl.pallas_call(basis_kernel, out_shape=(jax.ShapeDtypeStruct((COLS, 2, 8,...]
where the time goes in v5:
time: 55.7 us; the launch traced here: 55.5 us
  Pallas kernels  54.8 us (98%)
  between operations  0.64 us (1%)
    pallas_call x1, Pallas kernels, per_device(): pl.pallas_call(krylov_kernel, out_shape=(jax.ShapeDtypeStruct((CX, 2 * CO...  44.9 us
    pallas_call x1, Pallas kernels, per_device(): pl.pallas_call(basis_kernel, out_shape=(jax.ShapeDtypeStruct((COLS, 2, 8,...  9.96 us

profile of v5, /device:TPU:1, one launch (start us, length us, event | category | flops | bytes accessed | tf_op | source)
XLA Modules:
  0.0 55.5 jit_solution(15381591355998479816)
XLA Ops:
  0.6 44.9 %krylov.1 = (bf16[16,96,2048]{2,1,0:T(8,128)(2,1)}, f32[24,128]{1,0:T(8,128)}) custom-call(f32[16,2,8,2048]{3,2,1,0:T(8,128)} %bitcast.2, f32[16,2048]{1,0:T(8,128)} %cond.1, s32[16]{0:T(128)} %electrodes.1), custom_call_target="tpu_custom_call" | custom-call | tf_op jit(solution)/shard_map/krylov/pallas_call | solution.py:612
  45.5 10.0 %basis.1 = (f32[48,2,8,2048]{3,2,1,0:T(8,128)}, f32[48,48]{1,0:T(8,128)}) custom-call(bf16[16,96,2048]{2,1,0:T(8,128)(2,1)} %get-tuple-element.6.cols, f32[24,128]{1,0:T(8,128)} %get-tuple-element.7.gram), custom_call_target="tpu_custom_call" | custom-call | tf_op jit(solution)/shard_map/basis/pallas_call | solution.py:653

commit v6 on v4

--- a/solution.py
+++ b/solution.py
@@ -58,7 +58,6 @@
     electrodes,
     cols,
     gram,
-    natural,
     start,
     field,
     field_s,
@@ -96,26 +95,19 @@
     for move in MOVES:
         pl.semaphore_signal(barrier, inc=1, device_id=beside(move), device_id_type=MESH)
 
-    def load(half, t):
+    def load(x):
         return pltpu.make_async_copy(
-            guess.at[:, half, :, tile(t)],
-            natural.at[half, t].reshape(SRC, 8, LANES),
-            guess_sem.at[half, t],
+            guess.at[:, x, :], start.at[REACH + x, :, pl.ds(LANES, MERGED)], guess_sem.at[x]
         )
 
-    def each_load(act):
-        def step(t, carry):
-            for half in range(2):
-                act(load(half, t))
-            return carry
-
-        lax.fori_loop(0, TILES, step, 0)
-
+    faces = (*range(REACH), *range(CX - REACH, CX))
+    between = tuple(range(REACH, CX - REACH))
     load_cond = pltpu.make_async_copy(
         cond, cond_ext.at[pl.ds(8, CX), pl.ds(2 * LANES, MERGED)], local_sem.at[1]
     )
     load_cond.start()
-    each_load(lambda copy: copy.start())
+    for x in faces + between:
+        load(x).start()
     for kind, size in enumerate(GROUPS):
         for step in range(1, size):
             pl.semaphore_signal(
@@ -168,19 +160,8 @@
     for copy in cond_copies:
         copy.start()
 
-    each_load(lambda copy: copy.wait())
-
-    def lay_out(x, carry):
-        half, rest = x // 8, lax.rem(x, 8)
-        for t in range(TILES):
-            start[x + REACH, :, tile(t + 1)] = natural[half, t, pl.ds(rest, SRC, stride=8), :]
-        return carry
-
-    def lay_out_faces(x, carry):
-        lay_out(x, 0)
-        return lay_out(x + CX - REACH, carry)
-
-    lax.fori_loop(0, REACH, lay_out_faces, 0)
+    for x in faces:
+        load(x).wait()
 
     copies = []
     for i, (dx, dy) in enumerate(MOVES):
@@ -222,7 +203,8 @@
     for copy in along_x:
         copy.start()
 
-    lax.fori_loop(REACH, CX - REACH, lay_out, 0)
+    for x in between:
+        load(x).wait()
     lane = lax.broadcasted_iota(jnp.int32, (SRC, LANES), 1)
     low = lane < HALF
 
@@ -532,18 +514,15 @@
 
 def basis_kernel(cols, gram, basis, triangle, held, result, load_sem, store_sem):
     f32 = jnp.float32
-    chunks = 8
-    width = MERGED // chunks
-
-    def part(i):
-        lanes = pl.ds(pl.multiple_of(i * width, width), width)
-        return pltpu.make_async_copy(cols.at[:, :, lanes], held.at[:, :, lanes], load_sem.at[i])
-
-    def begin(i, carry):
-        part(i).start()
+
+    def load(x):
+        return pltpu.make_async_copy(cols.at[x], held.at[x], load_sem.at[x])
+
+    def begin(x, carry):
+        load(x).start()
         return carry
 
-    lax.fori_loop(0, chunks, begin, 0)
+    lax.fori_loop(0, CX, begin, 0)
 
     packed = gram[...]
     full = jnp.concatenate([packed, pltpu.roll(packed, HALF, 1)], axis=0)
@@ -593,37 +572,24 @@
     fine = (inverse - coarse.astype(f32)).astype(jnp.bfloat16)
     weights = jnp.concatenate([coarse, coarse, fine], axis=1)
 
-    per_chunk = width // LANES
-
-    def send(h, t):
-        return pltpu.make_async_copy(
-            result.at[h, t].reshape(COLS, 8, LANES), basis.at[:, h, :, tile(t)], store_sem.at[h, t]
-        )
-
-    def solve(i, carry):
-        part(i).wait()
-        lanes = pl.ds(pl.multiple_of(i * width, width), width)
-        for x in range(CX):
-            both = held[x, :, lanes]
-            stack = jnp.concatenate([both, both[:COLS]], axis=0)
-            solved = jnp.dot(weights, stack, preferred_element_type=f32)
-            for t in range(per_chunk):
-                result[x // 8, i * per_chunk + t, pl.ds(x % 8, COLS, stride=8), :] = solved[
-                    :, t * LANES : (t + 1) * LANES
-                ]
-        for h in range(2):
-            for t in range(per_chunk):
-                send(h, i * per_chunk + t).start()
+    def send(x):
+        return pltpu.make_async_copy(result.at[x], basis.at[:, x, :], store_sem.at[x])
+
+    def solve(x, carry):
+        load(x).wait()
+        both = held[x]
+        stack = jnp.concatenate([both, both[:COLS]], axis=0)
+        result[x] = jnp.dot(weights, stack, preferred_element_type=f32)
+        send(x).start()
         return carry
 
-    lax.fori_loop(0, chunks, solve, 0)
-
-    def finish(t, carry):
-        for h in range(2):
-            send(h, t).wait()
+    lax.fori_loop(0, CX, solve, 0)
+
+    def finish(x, carry):
+        send(x).wait()
         return carry
 
-    lax.fori_loop(0, TILES, finish, 0)
+    lax.fori_loop(0, CX, finish, 0)
 
 
 def per_device(initial_guess, conductivity, electrodes):
@@ -641,7 +607,6 @@
         in_specs=[any_space, any_space, smem],
         out_specs=(any_space, vmem),
         scratch_shapes=[
-            pltpu.VMEM((2, TILES, SRC * 8, LANES), f32),
             pltpu.VMEM((EXT_X, SRC, EXT), f32),
             pltpu.VMEM((EXT_X, SRC, EXT), f32),
             pltpu.VMEM((EXT_X, SRC, EXT), f32),
@@ -657,7 +622,7 @@
             pltpu.VMEM((GROUPS[0], COLS // 2, LANES), f32),
             pltpu.VMEM((GROUPS[1], COLS // 2, LANES), f32),
             pltpu.VMEM((GROUPS[2], COLS // 2, LANES), f32),
-            dma((2, TILES)),
+            dma((CX,)),
             dma((3,)),
             dma((8,)),
             dma((8,)),
@@ -672,25 +637,25 @@
             collective_id=0, has_side_effects=True, vmem_limit_bytes=60 * 2**20
         ),
         name="krylov",
-    )(initial_guess.reshape(SRC, 2, 8, MERGED), conductivity, electrodes)
+    )(initial_guess, conductivity, electrodes)
     basis, triangle = pl.pallas_call(
         basis_kernel,
         out_shape=(
-            jax.ShapeDtypeStruct((COLS, 2, 8, MERGED), f32),
+            jax.ShapeDtypeStruct((COLS, CX, MERGED), f32),
             jax.ShapeDtypeStruct((COLS, COLS), f32),
         ),
         in_specs=[any_space, vmem],
         out_specs=(any_space, vmem),
         scratch_shapes=[
             pltpu.VMEM((CX, 2 * COLS, MERGED), jnp.bfloat16),
-            pltpu.VMEM((2, TILES, COLS * 8, LANES), f32),
-            dma((8,)),
-            dma((2, TILES)),
+            pltpu.VMEM((CX, COLS, MERGED), f32),
+            dma((CX,)),
+            dma((CX,)),
         ],
         compiler_params=pltpu.CompilerParams(vmem_limit_bytes=60 * 2**20),
         name="basis",
     )(cols, gram)
-    return basis.reshape(COLS, CX, MERGED), triangle
+    return basis, triangle
 
 
 def solution(mesh):

time: 50.3 us -> 50.8 us (level)
    pallas_call x1, Pallas kernels: 8.34 us -> 9.25 us  [per_device(): pl.pallas_call(basis_kernel, out_shape=(jax.ShapeDtypeStruct((COLS, CX, M...]
where the time goes in v6:
time: 50.8 us; the launch traced here: 50.6 us
  Pallas kernels  50 us (98%)
  between operations  0.64 us (1%)
    pallas_call x1, Pallas kernels, per_device(): pl.pallas_call(krylov_kernel, out_shape=(jax.ShapeDtypeStruct((CX, 2 * CO...  40.7 us
    pallas_call x1, Pallas kernels, per_device(): pl.pallas_call(basis_kernel, out_shape=(jax.ShapeDtypeStruct((COLS, CX, M...  9.25 us

profile of v6, /device:TPU:1, one launch (start us, length us, event | category | flops | bytes accessed | tf_op | source)
XLA Modules:
  0.0 50.6 jit_solution(3348379815567434178)
XLA Ops:
  0.6 40.7 %krylov.1 = (bf16[16,96,2048]{2,1,0:T(8,128)(2,1)}, f32[24,128]{1,0:T(8,128)}) custom-call(f32[16,16,2048]{2,1,0:T(8,128)} %guess.1, f32[16,2048]{1,0:T(8,128)} %cond.1, s32[16]{0:T(128)} %electrodes.1), custom_call_target="tpu_custom_call" | custom-call | tf_op jit(solution)/shard_map/krylov/pallas_call | solution.py:601
  41.3 9.3 %basis.1 = (f32[48,16,2048]{2,1,0:T(8,128)}, f32[48,48]{1,0:T(8,128)}) custom-call(bf16[16,96,2048]{2,1,0:T(8,128)(2,1)} %get-tuple-element.4.cols, f32[24,128]{1,0:T(8,128)} %get-tuple-element.5.gram), custom_call_target="tpu_custom_call" | custom-call | tf_op jit(solution)/shard_map/basis/pallas_call | solution.py:641

commit v7 on v4

--- a/solution.py
+++ b/solution.py
@@ -58,7 +58,6 @@
     electrodes,
     cols,
     gram,
-    natural,
     start,
     field,
     field_s,
@@ -96,26 +95,19 @@
     for move in MOVES:
         pl.semaphore_signal(barrier, inc=1, device_id=beside(move), device_id_type=MESH)
 
-    def load(half, t):
+    def load(x):
         return pltpu.make_async_copy(
-            guess.at[:, half, :, tile(t)],
-            natural.at[half, t].reshape(SRC, 8, LANES),
-            guess_sem.at[half, t],
-        )
-
-    def each_load(act):
-        def step(t, carry):
-            for half in range(2):
-                act(load(half, t))
-            return carry
-
-        lax.fori_loop(0, TILES, step, 0)
-
+            guess.at[:, x, :], start.at[REACH + x, :, pl.ds(LANES, MERGED)], guess_sem.at[x]
+        )
+
+    faces = (*range(REACH), *range(CX - REACH, CX))
+    between = tuple(range(REACH, CX - REACH))
     load_cond = pltpu.make_async_copy(
         cond, cond_ext.at[pl.ds(8, CX), pl.ds(2 * LANES, MERGED)], local_sem.at[1]
     )
     load_cond.start()
-    each_load(lambda copy: copy.start())
+    for x in faces + between:
+        load(x).start()
     for kind, size in enumerate(GROUPS):
         for step in range(1, size):
             pl.semaphore_signal(
@@ -168,19 +160,8 @@
     for copy in cond_copies:
         copy.start()
 
-    each_load(lambda copy: copy.wait())
-
-    def lay_out(x, carry):
-        half, rest = x // 8, lax.rem(x, 8)
-        for t in range(TILES):
-            start[x + REACH, :, tile(t + 1)] = natural[half, t, pl.ds(rest, SRC, stride=8), :]
-        return carry
-
-    def lay_out_faces(x, carry):
-        lay_out(x, 0)
-        return lay_out(x + CX - REACH, carry)
-
-    lax.fori_loop(0, REACH, lay_out_faces, 0)
+    for x in faces:
+        load(x).wait()
 
     copies = []
     for i, (dx, dy) in enumerate(MOVES):
@@ -222,7 +203,8 @@
     for copy in along_x:
         copy.start()
 
-    lax.fori_loop(REACH, CX - REACH, lay_out, 0)
+    for x in between:
+        load(x).wait()
     lane = lax.broadcasted_iota(jnp.int32, (SRC, LANES), 1)
     low = lane < HALF
 
@@ -244,25 +226,23 @@
     for copy in cond_copies:
         copy.wait_recv()
     for i, x in enumerate((4, 8 + CX)):
-        cond_ext[pl.ds(x, 4), pl.ds(2 * LANES, MERGED)] = cond_in[i]
+        outside = (gx == 0, gx == GX - 1)[i]
+        cond_ext[pl.ds(x, 4), pl.ds(2 * LANES, MERGED)] = jnp.where(outside, 0.0, cond_in[i])
     row = lax.broadcasted_iota(jnp.int32, (CX + 16, LANES), 0)
     lane_c = lax.broadcasted_iota(jnp.int32, (CX + 16, LANES), 1)
     first_x, last_x = gx == 0, gx == GX - 1
     row_from = jnp.where(first_x, 8, 0)
     row_to = jnp.where(last_x, 8 + CX, 16 + CX)
-    inside_x = (row >= row_from) & (row < row_to)
-    tile_from = jnp.where(gy == 0, 2, 0)
-    tile_to = jnp.where(gy == GY - 1, TILES + 2, TILES + 4)
+    for t in (0, 1, TILES + 2, TILES + 3):
+        outside = gy == 0 if t < 2 else gy == GY - 1
+        kept = (row >= row_from) & (row < jnp.where(outside, 0, row_to))
+        cond_ext[:, tile(t)] = jnp.where(kept, cond_ext[:, tile(t)], 0.0)
     z = lax.rem(lane_c, HALF)
     low_c = lane_c < HALF
 
     def couplings(t, carry):
-        def load(place):
-            row_end = jnp.where((place >= tile_from) & (place < tile_to), row_to, 0)
-            return jnp.where(inside_x & (row < row_end), cond_ext[:, tile(place)], 0.0)
-
-        here = load(t + 1)
-        below, above = load(t), load(t + 2)
+        here = -0.5 * cond_ext[:, tile(t + 1)]
+        below, above = -0.5 * cond_ext[:, tile(t)], -0.5 * cond_ext[:, tile(t + 2)]
         swapped = swap_halves(here)
         outer = jnp.where(low_c, swap_halves(below), swap_halves(above))
         z_down = jnp.where(z == 0, 0.0, pltpu.roll(here, 1, 1))
@@ -272,9 +252,9 @@
         total = 6.0 * here
         for k, there in enumerate((x_down, x_up, swapped, outer, z_down, z_up)):
             total = total + there
-            face = jnp.where((here > 0.0) & (there > 0.0), -0.5 * (here + there), 0.0)
+            face = jnp.where(here * there > 0.0, here + there, 0.0)
             coef[t, pl.ds(k, CX + 16, stride=8), :] = face
-        coef[t, pl.ds(6, CX + 16, stride=8), :] = jnp.where(here > 0.0, 0.5 * total, 0.0)
+        coef[t, pl.ds(6, CX + 16, stride=8), :] = jnp.where(here < 0.0, -total, 0.0)
         return carry
 
     lax.fori_loop(0, EXT_T, couplings, 0)
@@ -641,7 +621,6 @@
         in_specs=[any_space, any_space, smem],
         out_specs=(any_space, vmem),
         scratch_shapes=[
-            pltpu.VMEM((2, TILES, SRC * 8, LANES), f32),
             pltpu.VMEM((EXT_X, SRC, EXT), f32),
             pltpu.VMEM((EXT_X, SRC, EXT), f32),
             pltpu.VMEM((EXT_X, SRC, EXT), f32),
@@ -657,7 +636,7 @@
             pltpu.VMEM((GROUPS[0], COLS // 2, LANES), f32),
             pltpu.VMEM((GROUPS[1], COLS // 2, LANES), f32),
             pltpu.VMEM((GROUPS[2], COLS // 2, LANES), f32),
-            dma((2, TILES)),
+            dma((CX,)),
             dma((3,)),
             dma((8,)),
             dma((8,)),
@@ -672,7 +651,7 @@
             collective_id=0, has_side_effects=True, vmem_limit_bytes=60 * 2**20
         ),
         name="krylov",
-    )(initial_guess.reshape(SRC, 2, 8, MERGED), conductivity, electrodes)
+    )(initial_guess, conductivity, electrodes)
     basis, triangle = pl.pallas_call(
         basis_kernel,
         out_shape=(

time: 50.3 us -> 49.8 us (0.990)
  no operation moved by 1% of the time
where the time goes in v7:
time: 49.8 us; the launch traced here: 49.7 us
  Pallas kernels  49 us (98%)
  between operations  0.64 us (1%)
    pallas_call x1, Pallas kernels, per_device(): pl.pallas_call(krylov_kernel, out_shape=(jax.ShapeDtypeStruct((CX, 2 * CO...  40.7 us
    pallas_call x1, Pallas kernels, per_device(): pl.pallas_call(basis_kernel, out_shape=(jax.ShapeDtypeStruct((COLS, 2, 8,...  8.34 us

profile of v7, /device:TPU:1, one launch (start us, length us, event | category | flops | bytes accessed | tf_op | source)
XLA Modules:
  0.0 49.7 jit_solution(17717235766858909962)
XLA Ops:
  0.6 40.7 %krylov.1 = (bf16[16,96,2048]{2,1,0:T(8,128)(2,1)}, f32[24,128]{1,0:T(8,128)}) custom-call(f32[16,16,2048]{2,1,0:T(8,128)} %guess.1, f32[16,2048]{1,0:T(8,128)} %cond.1, s32[16]{0:T(128)} %electrodes.1), custom_call_target="tpu_custom_call" | custom-call | tf_op jit(solution)/shard_map/krylov/pallas_call | solution.py:615
  41.3 8.3 %basis.1 = (f32[48,2,8,2048]{3,2,1,0:T(8,128)}, f32[48,48]{1,0:T(8,128)}) custom-call(bf16[16,96,2048]{2,1,0:T(8,128)(2,1)} %get-tuple-element.6.cols, f32[24,128]{1,0:T(8,128)} %get-tuple-element.7.gram), custom_call_target="tpu_custom_call" | custom-call | tf_op jit(solution)/shard_map/basis/pallas_call | solution.py:655

commit v8 on v7

--- a/solution.py
+++ b/solution.py
@@ -487,7 +487,7 @@
         me = place(kind, gx, gy)
         part[me] = total
         sums = []
-        for step in range(1, size):
+        for step in sorted(range(1, size), key=lambda n: abs(2 * n - size)):
             copy = pltpu.make_async_remote_copy(
                 src_ref=part.at[me],
                 dst_ref=part.at[me],

time: 49.8 us -> 49 us (0.984)
  Pallas kernels: 49 us -> 47.9 us
    pallas_call x1, Pallas kernels: 40.7 us -> 39.5 us  [per_device(): pl.pallas_call(krylov_kernel, out_shape=(jax.ShapeDtypeStruct((CX, 2 * CO...]
where the time goes in v8:
time: 49 us; the launch traced here: 48.5 us
  Pallas kernels  47.9 us (98%)
  between operations  0.64 us (1%)
    pallas_call x1, Pallas kernels, per_device(): pl.pallas_call(krylov_kernel, out_shape=(jax.ShapeDtypeStruct((CX, 2 * CO...  39.5 us
    pallas_call x1, Pallas kernels, per_device(): pl.pallas_call(basis_kernel, out_shape=(jax.ShapeDtypeStruct((COLS, 2, 8,...  8.34 us

profile of v8, /device:TPU:1, one launch (start us, length us, event | category | flops | bytes accessed | tf_op | source)
XLA Modules:
  0.0 48.5 jit_solution(10720570254454601454)
XLA Ops:
  0.6 39.5 %krylov.1 = (bf16[16,96,2048]{2,1,0:T(8,128)(2,1)}, f32[24,128]{1,0:T(8,128)}) custom-call(f32[16,16,2048]{2,1,0:T(8,128)} %guess.1, f32[16,2048]{1,0:T(8,128)} %cond.1, s32[16]{0:T(128)} %electrodes.1), custom_call_target="tpu_custom_call" | custom-call | tf_op jit(solution)/shard_map/krylov/pallas_call | solution.py:615
  40.2 8.3 %basis.1 = (f32[48,2,8,2048]{3,2,1,0:T(8,128)}, f32[48,48]{1,0:T(8,128)}) custom-call(bf16[16,96,2048]{2,1,0:T(8,128)(2,1)} %get-tuple-element.6.cols, f32[24,128]{1,0:T(8,128)} %get-tuple-element.7.gram), custom_call_target="tpu_custom_call" | custom-call | tf_op jit(solution)/shard_map/basis/pallas_call | solution.py:655
